TPU v7x, 512 devices: a whole 4x4x16 slice. The times are simulated.
512 devices in a mesh: grp: 16 (over y, z_hi), row: 32 (over z_lo, x, core).
Axes of the slice: x: 4, y: 4, z: 16 (z_hi: 4, z_lo: 4; z = z_hi * 4 + z_lo), core: 2. Of those that a mesh axis runs over, the one named last changes fastest.
Arguments:
- integrals: bfloat16 [16, 6144, 6144], P('grp', 'row'), may hold values from -6 to 6
- occupied: bfloat16 [6144, 512], P('row'), may hold values from -0.0078125 to 0.0078125
Outputs:
- exchange_matrix: float32 [6144, 6144], P('row', 'grp')
All inputs are finite; a program needn't handle non-finite values.
Results may differ from a plain program's by a relative error of at most 0.015.
Values may be sent and summed in bfloat16 or wider, within the bound.
A program may use at most 64 MiB of HBM per device.

v0:
```python
import jax
import jax.numpy as jnp
from jax import lax
from jax.sharding import PartitionSpec as P


def local(integrals, occupied):
    aux_local, mu_rows, basis_width = integrals.shape
    occ_width = occupied.shape[1]
    flattened = integrals.reshape(aux_local * mu_rows, basis_width)
    transformed = jnp.dot(
        flattened,
        lax.all_gather(occupied, "row", axis=0, tiled=True),
        preferred_element_type=jnp.float32,
    )
    half_rows = transformed.astype(jnp.bfloat16).reshape(aux_local, mu_rows, occ_width)
    half_rows = jnp.transpose(half_rows, (1, 0, 2)).reshape(mu_rows, aux_local * occ_width)
    product_block = lax.dot_general(
        half_rows,
        lax.all_gather(half_rows, "row", axis=0, tiled=True),
        (((1,), (1,)), ((), ())),
        preferred_element_type=jnp.float32,
    )
    return lax.psum_scatter(
        product_block.astype(jnp.bfloat16), "grp", scatter_dimension=1, tiled=True
    ).astype(jnp.float32)


def solution(mesh):
    in_specs = (P("grp", "row", None), P("row", None))
    out_specs = P("row", "grp")
    return jax.shard_map(local, mesh=mesh, in_specs=in_specs, out_specs=out_specs, check_vma=False)
```

profile of v0, /device:TPU:1, one launch (start us, length us, event | category | flops | bytes accessed | tf_op | source)
XLA Modules:
  0.0 323.1 jit_solution(9176689323916349126)
XLA Ops:
  6.5 0.0 copy-start
  6.5 0.0 all-gather.3.cloned.1.call-start
  6.5 0.7 all-gather.3.cloned.1.call-update
  7.3 0.0 all-gather.5.cloned.1.call-start
  7.3 79.4 %all-gather.3.cloned.1.call-done = bf16[6144,512]{1,0:T(8,128)(2,1)} async-done(((bf16[192,512]{1,0:T(8,128)(2,1)}), bf16[6144,512]{1,0:T(8,128)(2,1)}) %all-gather.3.cloned.1.call-update) | async-done | bytes 6291472 | tf_op jit(solution)/shard_map/all_gather | solution.py:13
  86.7 0.0 copy-done
  86.7 4.8 %fusion.2 = bf16[192,512]{1,0:T(8,128)(2,1)} fusion(bf16[6144,512]{1,0:T(8,128)(2,1)} %all-gather.3.cloned.1.call-done, bf16[1,192,6144]{2,1,0:T(8,128)(2,1)S(1)} %copy-done), kind=kOutput, calls=%fused_computation.3 | convolution fusion | flops 1208057856 | bytes 8847360 | tf_op jit(solution)/shard_map/dot_general | solution.py:11
  91.6 0.0 all-gather.5.cloned.1.call-update
  91.6 0.0 reduce-scatter.4.cloned.1.call-start
  91.7 70.7 %all-gather.5.cloned.1.call-done = bf16[6144,512]{1,0:T(8,128)(2,1)} async-done(((bf16[192,512]{1,0:T(8,128)(2,1)}), bf16[6144,512]{1,0:T(8,128)(2,1)}) %all-gather.5.cloned.1.call-update) | async-done | bytes 6291472 | tf_op jit(solution)/shard_map/all_gather | solution.py:20
  162.4 6.5 %convolution_convert_fusion = bf16[192,6144]{1,0:T(8,128)(2,1)} fusion(bf16[192,512]{1,0:T(8,128)(2,1)} %fusion.2, bf16[6144,512]{1,0:T(8,128)(2,1)} %all-gather.5.cloned.1.call-done), kind=kOutput, calls=%fused_computation | convolution fusion | flops 1209139200 | bytes 8847360 | tf_op jit(solution)/shard_map/dot_general | solution.py:18
  168.9 4.5 %copy.3 = bf16[192,6144]{0,1:T(8,128)(2,1)} copy(bf16[192,6144]{1,0:T(8,128)(2,1)} %convolution_convert_fusion) | data formatting | bytes 4718592
  173.4 0.0 reduce-scatter.4.cloned.1.call-update
  173.4 141.3 %reduce-scatter.4.cloned.1.call-done = bf16[384,192]{1,0:T(8,128)(2,1)} async-done(((bf16[6144,192]{1,0:T(8,128)(2,1)}), bf16[384,192]{1,0:T(8,128)(2,1)}) %reduce-scatter.4.cloned.1.call-update) | async-done | bytes 147472
  314.8 1.1 copy.4
  315.8 0.7 convert_element_type.11
Async XLA Ops:
  6.5 80.2 %copy-start = (bf16[1,192,6144]{2,1,0:T(8,128)(2,1)S(1)}, bf16[1,192,6144]{2,1,0:T(8,128)(2,1)}, u32[]{:S(2)}) copy-start(bf16[1,192,6144]{2,1,0:T(8,128)(2,1)} %param.2) | copy-start | bytes 7077892
  6.5 80.2 %all-gather.3.cloned.1.call-start = ((), (), s32[]{:S(2)}) async-start(), calls=%async_computation.1 | async-start | bytes 6488064 | tf_op jit(solution)/shard_map/all_gather | solution.py:13
  7.3 155.1 %all-gather.5.cloned.1.call-start = ((), (), s32[]{:S(2)}) async-start(), calls=%async_computation.2 | async-start | bytes 6488064 | tf_op jit(solution)/shard_map/all_gather | solution.py:20
  91.6 223.1 %reduce-scatter.4.cloned.1.call-start = ((), (), s32[]{:S(2)}) async-start(), calls=%async_computation.3 | async-start | bytes 3342336
Sparse Core Ops, SparseCore 0:
  9.5 77.1 all-gather.2
  91.7 70.5 all-gather.4
  173.5 141.1 reduce-scatter.3
where the time goes:
time: 324 us; the launch traced here: 323 us
  waiting for transfers between devices  292 us (90%)
  between operations  13.1 us (4%)
  matrix products  11.4 us (4%)
  local copies, waits for them, and re-layouts  5.55 us (2%)
    unnamed x4, waiting for transfers between devices  142 us
    all_gather x1, waiting for transfers between devices, local(): lax.all_gather(occupied, 'row', axis=0, tiled=True)  79.4 us
    all_gather x1, waiting for transfers between devices, local(): lax.all_gather(half_rows, 'row', axis=0, tiled=True)  70.7 us
    dot_general x1, matrix products, local(): lax.dot_general(half_rows, lax.all_gather(half_rows, 'row', axis=0, tiled...  6.54 us
  transfers between devices with their start and end apart: 3, of which 3 were waited for; matrix products, arithmetic and copies ran while one was open for 0% of the time, Pallas kernels for 0%

commit v1 on v0

v1 whole, which is shorter than its diff:
```python
import jax
import jax.numpy as jnp
from jax import lax
from jax.experimental import pallas as pl
from jax.experimental.pallas import tpu as pltpu
from jax.sharding import PartitionSpec as P

MESH = pl.DeviceIdType.MESH
F32 = jnp.float32
BF16 = jnp.bfloat16

N_SEM = 192


def kernel(ints_hbm, occ_hbm, out_ref, occ, ints, hacc, hrow, hcol, pb,
           yin, ysum, xin, zin, zbuf, ssem, rsem, lsem):
    grp, row = lax.axis_index("grp"), lax.axis_index("row")
    y, zh = grp // 4, grp % 4
    zl, x, c = row // 8, (row // 2) % 4, row % 2
    z = zh * 4 + zl

    def up(v, d, n=4):
        return (v + d + n) % n

    def at(dx=0, dy=0, dz=0):
        zz = up(z, dz, 16)
        return (up(y, dy) * 4 + zz // 4, (zz % 4) * 8 + up(x, dx) * 2 + c)

    def in_group(d):
        return (grp, up(zl, d) * 8 + x * 2 + c)

    sibling = (grp, zl * 8 + x * 2 + (1 - c))

    copies = []

    def send(src, dst, to):
        k = len(copies)
        copy = pltpu.make_async_remote_copy(
            src_ref=src, dst_ref=dst, send_sem=ssem.at[k], recv_sem=rsem.at[k],
            device_id=to, device_id_type=MESH)
        copy.start()
        copies.append(copy)
        return copy

    def same(ref, to):
        return send(ref, ref, to)

    own_copy = pltpu.make_async_copy(occ_hbm, occ.at[zl, x, c], lsem.at[0])
    own_copy.start()
    ints_copy = pltpu.make_async_copy(ints_hbm, ints, lsem.at[1])
    ints_copy.start()

    barrier = pltpu.get_barrier_semaphore()
    partners = [sibling, at(dx=1), at(dx=2), at(dx=-1), at(dy=1), at(dy=-1), at(dz=1), at(dz=-1),
                at(dz=4), at(dz=-4), in_group(1), in_group(2), in_group(3)]
    for partner in partners:
        pl.semaphore_signal(barrier, inc=1, device_id=partner, device_id_type=MESH)
    pl.semaphore_wait(barrier, len(partners))
    own_copy.wait()

    xr, xl, xo = up(x, 1), up(x, -1), up(x, 2)
    zr, zd, zo = up(zl, 1), up(zl, -1), up(zl, 2)
    east, west, north, south = at(dx=1), at(dx=-1), at(dz=1), at(dz=-1)
    PA, PB = pl.ds(0, 256), pl.ds(256, 256)
    ALL, TOP, BOT = pl.ds(0, 192), pl.ds(0, 96), pl.ds(96, 96)

    def blk(bz, bx, rows, cols):
        return occ.at[bz, bx, c, rows, cols]

    fwd_a = [[], []]
    fwd_b = [[], []]
    own_a, own_b = blk(zl, x, ALL, PA), blk(zl, x, ALL, PB)
    a_e, a_w = same(own_a, east), same(own_a, west)
    b_n, b_s = same(own_b, north), same(own_b, south)
    fwd_a[0].append(same(own_a, north))
    fwd_a[1].append(same(own_a, south))
    fwd_b[0].append(same(own_b, east))
    fwd_b[1].append(same(own_b, west))
    sib_own = same(occ.at[zl, x, c], sibling)

    a_e.wait_recv()
    a_et = same(blk(zl, xl, TOP, PA), east)
    fwd_a[0].append(same(blk(zl, xl, ALL, PA), north))
    fwd_a[1].append(same(blk(zl, xl, ALL, PA), south))
    b_n.wait_recv()
    b_nt = same(blk(zd, x, TOP, PB), north)
    fwd_b[0].append(same(blk(zd, x, ALL, PB), east))
    fwd_b[1].append(same(blk(zd, x, ALL, PB), west))
    a_w.wait_recv()
    a_wb = same(blk(zl, xr, BOT, PA), west)
    fwd_a[0].append(same(blk(zl, xr, ALL, PA), north))
    fwd_a[1].append(same(blk(zl, xr, ALL, PA), south))
    b_s.wait_recv()
    b_sb = same(blk(zr, x, BOT, PB), south)
    fwd_b[0].append(same(blk(zr, x, ALL, PB), east))
    fwd_b[1].append(same(blk(zr, x, ALL, PB), west))
    sib_a0 = [sib_own, same(blk(zl, xl, ALL, PA), sibling), same(blk(zl, xr, ALL, PA), sibling)]
    sib_b0 = [same(blk(zd, x, ALL, PB), sibling), same(blk(zr, x, ALL, PB), sibling)]
    a_et.wait_recv()
    a_wb.wait_recv()
    fwd_a[0].append(same(blk(zl, xo, ALL, PA), north))
    fwd_a[1].append(same(blk(zl, xo, ALL, PA), south))
    sib_a0.append(same(blk(zl, xo, ALL, PA), sibling))
    b_nt.wait_recv()
    b_sb.wait_recv()
    fwd_b[0].append(same(blk(zo, x, ALL, PB), east))
    fwd_b[1].append(same(blk(zo, x, ALL, PB), west))
    sib_b0.append(same(blk(zo, x, ALL, PB), sibling))

    last_a, last_b = [], []
    sib_a1, sib_b1 = [], []
    for bx, bz, j in zip((x, xl, xr, xo), (zl, zd, zr, zo), range(4)):
        fwd_a[0][j].wait_recv()
        t = same(blk(zd, bx, TOP, PA), north)
        sib_a1.append(same(blk(zd, bx, ALL, PA), sibling))
        fwd_a[1][j].wait_recv()
        u = same(blk(zr, bx, BOT, PA), south)
        sib_a1.append(same(blk(zr, bx, ALL, PA), sibling))
        last_a.append((t, u, bx))
        fwd_b[0][j].wait_recv()
        t = same(blk(bz, xl, TOP, PB), east)
        sib_b1.append(same(blk(bz, xl, ALL, PB), sibling))
        fwd_b[1][j].wait_recv()
        u = same(blk(bz, xr, BOT, PB), west)
        sib_b1.append(same(blk(bz, xr, ALL, PB), sibling))
        last_b.append((t, u, bz))

    def lanes(start, size):
        return pl.ds(pl.multiple_of(start, 128), size)

    def part_a(bz):
        return jnp.dot(ints[:, lanes(bz * 1536, 1536)],
                       occ[bz, :, :, :, 0:256].reshape(1536, 256), preferred_element_type=F32)

    def part_b(bx):
        total = None
        for bz in range(4):
            term = jnp.dot(ints[:, lanes(bz * 1536 + bx * 384, 384)],
                           occ[bz, bx, :, :, 256:512].reshape(384, 256), preferred_element_type=F32)
            total = term if total is None else total + term
        return total

    ints_copy.wait()
    for copy in sib_a0 + sib_b0:
        copy.wait_recv()
    hacc[:, 0:256] = part_a(zl)
    hacc[:, 256:512] = part_b(x)
    for copy in sib_a1 + sib_b1:
        copy.wait_recv()
    hacc[:, 0:256] += part_a(zd)
    hacc[:, 256:512] += part_b(xl)
    hacc[:, 0:256] += part_a(zr)
    hacc[:, 256:512] += part_b(xr)
    sib_2 = []
    for (t, u, bx), (v, w, bz) in zip(last_a, last_b):
        t.wait_recv()
        u.wait_recv()
        sib_2.append(same(blk(zo, bx, ALL, PA), sibling))
        v.wait_recv()
        w.wait_recv()
        sib_2.append(same(blk(bz, xo, ALL, PB), sibling))
    for copy in sib_2:
        copy.wait_recv()
    h_a = (hacc[:, 0:256] + part_a(zo)).astype(BF16)
    h_b = (hacc[:, 256:512] + part_b(xo)).astype(BF16)
    hrow[x, :, 0:256] = h_a
    hrow[x, :, 256:512] = h_b
    for s in range(3):
        hcol[s, zl, c, :, 0:256] = h_a[64 * s:64 * s + 64]
        hcol[s, zl, c, :, 256:512] = h_b[64 * s:64 * s + 64]

    r_e, r_w = same(hrow.at[x], east), same(hrow.at[x], west)
    c_in = []
    for s in range(3):
        c_in.append([same(hcol.at[s, zl, c], in_group(d)) for d in (1, 3, 2)])
    c_sib = [[same(hcol.at[s, zl, c], sibling)] for s in range(3)]
    r_e.wait_recv()
    r_et = same(hrow.at[xl, TOP], east)
    r_w.wait_recv()
    r_wb = same(hrow.at[xr, BOT], west)

    yr, yl, yo = up(y, 1), up(y, -1), up(y, 2)
    y_up, y_dn = at(dy=1), at(dy=-1)
    hr, hl, ho = up(zh, 1), up(zh, -1), up(zh, 2)
    z_up, z_dn = at(dz=4), at(dz=-4)
    A, B = pl.ds(0, 384), pl.ds(384, 384)
    TA, TB = pl.ds(0, 96), pl.ds(96, 96)
    y1, y2, xs, z1, z2 = {}, {}, {}, {}, {}

    def columns_in(s):
        for copy, d in zip(c_in[s], (3, 1, 2)):
            copy.wait_recv()
            c_sib[s].append(same(hcol.at[s, up(zl, d), c], sibling))
        for copy in c_sib[s]:
            copy.wait_recv()

    def product(s):
        for half in range(2):
            cols = hcol[s, 2 * half:2 * half + 2].reshape(256, 512)
            for bx in range(4):
                p = lax.dot_general(hrow[bx], cols, (((1,), (1,)), ((), ())), preferred_element_type=F32)
                p = p.astype(BF16)
                pb[s, 2 * half, 192 * bx:192 * bx + 192] = p[:, 0:128]
                pb[s, 2 * half + 1, 192 * bx:192 * bx + 192] = p[:, 128:256]

    def y_first(s):
        y1[s] = (send(pb.at[s, yo, A], yin.at[s, 0], y_up),
                 send(pb.at[s, yo, B], yin.at[s, 1], y_dn),
                 send(pb.at[s, yr, B], yin.at[s, 2], y_up),
                 send(pb.at[s, yl, A], yin.at[s, 3], y_dn))

    def y_second(s):
        y1[s][0].wait_recv()
        pb[s, yr, A] = (pb[s, yr, A].astype(F32) + yin[s, 0].astype(F32)).astype(BF16)
        up_copy = send(pb.at[s, yr, A], yin.at[s, 4], y_up)
        y1[s][1].wait_recv()
        pb[s, yl, B] = (pb[s, yl, B].astype(F32) + yin[s, 1].astype(F32)).astype(BF16)
        y2[s] = (up_copy, send(pb.at[s, yl, B], yin.at[s, 5], y_dn))

    def y_last(s):
        for copy in y1[s][2:] + y2[s]:
            copy.wait_recv()
        ysum[s, 0:2] = (pb[s, y, A].astype(F32) + yin[s, 3].astype(F32)
                        + yin[s, 4].astype(F32)).astype(BF16).reshape(2, 192, 128)
        ysum[s, 2:4] = (pb[s, y, B].astype(F32) + yin[s, 2].astype(F32)
                        + yin[s, 5].astype(F32)).astype(BF16).reshape(2, 192, 128)
        xs[s] = [send(ysum.at[s, up(x, d)], xin.at[s, x], at(dx=d)) for d in (2, 1, -1)]
        xin[s, x] = ysum[s, x]

    def z_first(s):
        for copy in xs[s]:
            copy.wait_recv()
        z1[s] = (send(xin.at[s, ho, TA], zin.at[s, 0], z_up),
                 send(xin.at[s, ho, TB], zin.at[s, 1], z_dn),
                 send(xin.at[s, hr, TB], zin.at[s, 2], z_up),
                 send(xin.at[s, hl, TA], zin.at[s, 3], z_dn))

    def z_second(s):
        z1[s][0].wait_recv()
        zbuf[s, 0] = (xin[s, hr, TA].astype(F32) + zin[s, 0].astype(F32)).astype(BF16)
        up_copy = send(zbuf.at[s, 0], zin.at[s, 4], z_up)
        z1[s][1].wait_recv()
        zbuf[s, 1] = (xin[s, hl, TB].astype(F32) + zin[s, 1].astype(F32)).astype(BF16)
        z2[s] = (up_copy, send(zbuf.at[s, 1], zin.at[s, 5], z_dn))

    def z_last(s):
        for copy in z1[s][2:] + z2[s]:
            copy.wait_recv()
        top = xin[s, zh, TA].astype(F32) + zin[s, 3].astype(F32) + zin[s, 4].astype(F32)
        bot = xin[s, zh, TB].astype(F32) + zin[s, 2].astype(F32) + zin[s, 5].astype(F32)
        for rows, v in ((slice(0, 96), top), (slice(96, 192), bot)):
            out_ref[rows, 64 * s:64 * s + 64] = v[:, 0:64]
            out_ref[rows, 192 + 64 * s:192 + 64 * s + 64] = v[:, 64:128]

    columns_in(0)
    r_et.wait_recv()
    r_wb.wait_recv()
    product(0)
    y_first(0)
    columns_in(1)
    product(1)
    y_second(0)
    y_first(1)
    columns_in(2)
    product(2)
    y_second(1)
    y_first(2)
    y_last(0)
    y_second(2)
    z_first(0)
    y_last(1)
    z_second(0)
    z_first(1)
    y_last(2)
    z_second(1)
    z_last(0)
    z_first(2)
    z_last(1)
    z_second(2)
    z_last(2)
    for copy in copies:
        copy.wait_send()


def local(integrals, occupied):
    return pl.pallas_call(
        kernel,
        out_shape=jax.ShapeDtypeStruct((192, 384), F32),
        in_specs=[pl.BlockSpec(memory_space=pl.ANY)] * 2,
        out_specs=pl.BlockSpec(memory_space=pltpu.VMEM),
        scratch_shapes=[
            pltpu.VMEM((4, 4, 2, 192, 512), BF16),
            pltpu.VMEM((192, 6144), BF16),
            pltpu.VMEM((192, 512), F32),
            pltpu.VMEM((4, 192, 512), BF16),
            pltpu.VMEM((3, 4, 2, 64, 512), BF16),
            pltpu.VMEM((3, 4, 768, 128), BF16),
            pltpu.VMEM((3, 6, 384, 128), BF16),
            pltpu.VMEM((3, 4, 192, 128), BF16),
            pltpu.VMEM((3, 4, 192, 128), BF16),
            pltpu.VMEM((3, 6, 96, 128), BF16),
            pltpu.VMEM((3, 2, 96, 128), BF16),
            pltpu.SemaphoreType.DMA((N_SEM,)),
            pltpu.SemaphoreType.DMA((N_SEM,)),
            pltpu.SemaphoreType.DMA((2,)),
        ],
        compiler_params=pltpu.CompilerParams(
            collective_id=0, has_side_effects=True, vmem_limit_bytes=48 << 20),
        name="exchange",
    )(integrals.reshape(192, 6144), occupied)


def solution(mesh):
    in_specs = (P("grp", "row", None), P("row", None))
    return jax.shard_map(local, mesh=mesh, in_specs=in_specs, out_specs=P("row", "grp"), check_vma=False)
```

time: 324 us -> 104 us (0.32)
  the two profiles are of different devices: /device:TPU:1 before, /device:TPU:24 now
where the time goes in v1:
time: 104 us
  Pallas kernels  100 us (96%)
  local copies, waits for them, and re-layouts  3.31 us (3%)
    pallas_call x1, Pallas kernels, local(): pl.pallas_call(kernel, out_shape=jax.ShapeDtypeStruct((192, 384), F32), i...  100 us
    unnamed x5, local copies, waits for them, and re-layouts  3.31 us

profile of v1, /device:TPU:24, one launch (start us, length us, event | category | flops | bytes accessed | tf_op | source)
XLA Modules:
  0.0 103.6 jit_solution(6760964572604358915)
XLA Ops:
  0.0 0.0 copy-start
  0.0 1.7 %copy-done = bf16[1,192,6144]{2,1,0:T(8,128)(2,1)S(1)} copy-done((bf16[1,192,6144]{2,1,0:T(8,128)(2,1)S(1)}, bf16[1,192,6144]{2,1,0:T(8,128)(2,1)}, u32[]{:S(2)}) %copy-start) | copy-done | bytes 2359320
  1.7 0.0 copy-start.1
  1.7 0.9 copy-done.1
  2.6 100.3 %exchange.1 = f32[192,384]{1,0:T(8,128)S(1)} custom-call(bf16[192,6144]{1,0:T(8,128)(2,1)S(1)} %bitcast.1, bf16[192,512]{1,0:T(8,128)(2,1)S(1)} %copy-done.1), custom_call_target="tpu_custom_call" | custom-call | tf_op jit(solution)/shard_map/exchange/pallas_call | solution.py:286
  102.9 0.7 copy.4
Async XLA Ops:
  0.0 1.7 %copy-start = (bf16[1,192,6144]{2,1,0:T(8,128)(2,1)S(1)}, bf16[1,192,6144]{2,1,0:T(8,128)(2,1)}, u32[]{:S(2)}) copy-start(bf16[1,192,6144]{2,1,0:T(8,128)(2,1)} %param.2) | copy-start | bytes 7077892
  1.7 0.9 copy-start.1

commit v2 on v1

--- a/solution.py
+++ b/solution.py
@@ -257,18 +257,18 @@
     r_wb.wait_recv()
     product(0)
     y_first(0)
+    y_second(0)
     columns_in(1)
     product(1)
-    y_second(0)
     y_first(1)
+    y_last(0)
+    y_second(1)
     columns_in(2)
     product(2)
-    y_second(1)
     y_first(2)
-    y_last(0)
-    y_second(2)
     z_first(0)
     y_last(1)
+    y_second(2)
     z_second(0)
     z_first(1)
     y_last(2)
@@ -305,7 +305,7 @@
             pltpu.SemaphoreType.DMA((2,)),
         ],
         compiler_params=pltpu.CompilerParams(
-            collective_id=0, has_side_effects=True, vmem_limit_bytes=48 << 20),
+            collective_id=0, has_side_effects=True, vmem_limit_bytes=60 << 20),
         name="exchange",
     )(integrals.reshape(192, 6144), occupied)
 

time: 104 us -> 94.7 us (0.911)
  the two profiles are of different devices: /device:TPU:24 before, /device:TPU:1 now
where the time goes in v2:
time: 94.7 us; the launch traced here: 94.6 us
  Pallas kernels  92.9 us (98%)
  local copies, waits for them, and re-layouts  1.69 us (2%)
    pallas_call x1, Pallas kernels, local(): pl.pallas_call(kernel, out_shape=jax.ShapeDtypeStruct((192, 384), F32), i...  92.9 us

profile of v2, /device:TPU:1, one launch (start us, length us, event | category | flops | bytes accessed | tf_op | source)
XLA Modules:
  0.0 94.6 jit_solution(12047183605445156696)
XLA Ops:
  0.0 92.9 %exchange.1 = f32[192,384]{1,0:T(8,128)} custom-call(bf16[192,6144]{1,0:T(8,128)(2,1)} %bitcast.1, bf16[192,512]{1,0:T(8,128)(2,1)} %occ_hbm.1), custom_call_target="tpu_custom_call" | custom-call | tf_op jit(solution)/shard_map/exchange/pallas_call | solution.py:286
  92.9 1.7 %copy.4 = f32[192,384]{1,0:T(8,128)} copy(f32[192,384]{1,0:T(8,128)} %exchange.1) | data formatting | bytes 589824

commit v3 on v1

--- a/solution.py
+++ b/solution.py
@@ -169,10 +169,13 @@
         hcol[s, zl, c, :, 0:256] = h_a[64 * s:64 * s + 64]
         hcol[s, zl, c, :, 256:512] = h_b[64 * s:64 * s + 64]
 
-    r_e, r_w = same(hrow.at[x], east), same(hrow.at[x], west)
-    c_in = []
-    for s in range(3):
-        c_in.append([same(hcol.at[s, zl, c], in_group(d)) for d in (1, 3, 2)])
+    def columns_out(s):
+        return [same(hcol.at[s, zl, c], in_group(d)) for d in (1, 3, 2)]
+
+    r_e, r_w = same(hrow.at[x, TOP], east), same(hrow.at[x, BOT], west)
+    c_in = [columns_out(0)]
+    r_e2, r_w2 = same(hrow.at[x, BOT], east), same(hrow.at[x, TOP], west)
+    c_in += [columns_out(1), columns_out(2)]
     c_sib = [[same(hcol.at[s, zl, c], sibling)] for s in range(3)]
     r_e.wait_recv()
     r_et = same(hrow.at[xl, TOP], east)
@@ -183,8 +186,8 @@
     y_up, y_dn = at(dy=1), at(dy=-1)
     hr, hl, ho = up(zh, 1), up(zh, -1), up(zh, 2)
     z_up, z_dn = at(dz=4), at(dz=-4)
-    A, B = pl.ds(0, 384), pl.ds(384, 384)
-    TA, TB = pl.ds(0, 96), pl.ds(96, 96)
+    A, B = pl.ds(0, 192), pl.ds(192, 192)
+    TA, TB = pl.ds(0, 48), pl.ds(48, 48)
     y1, y2, xs, z1, z2 = {}, {}, {}, {}, {}
 
     def columns_in(s):
@@ -200,84 +203,72 @@
             for bx in range(4):
                 p = lax.dot_general(hrow[bx], cols, (((1,), (1,)), ((), ())), preferred_element_type=F32)
                 p = p.astype(BF16)
-                pb[s, 2 * half, 192 * bx:192 * bx + 192] = p[:, 0:128]
-                pb[s, 2 * half + 1, 192 * bx:192 * bx + 192] = p[:, 128:256]
-
-    def y_first(s):
-        y1[s] = (send(pb.at[s, yo, A], yin.at[s, 0], y_up),
-                 send(pb.at[s, yo, B], yin.at[s, 1], y_dn),
-                 send(pb.at[s, yr, B], yin.at[s, 2], y_up),
-                 send(pb.at[s, yl, A], yin.at[s, 3], y_dn))
-
-    def y_second(s):
-        y1[s][0].wait_recv()
-        pb[s, yr, A] = (pb[s, yr, A].astype(F32) + yin[s, 0].astype(F32)).astype(BF16)
-        up_copy = send(pb.at[s, yr, A], yin.at[s, 4], y_up)
-        y1[s][1].wait_recv()
-        pb[s, yl, B] = (pb[s, yl, B].astype(F32) + yin[s, 1].astype(F32)).astype(BF16)
-        y2[s] = (up_copy, send(pb.at[s, yl, B], yin.at[s, 5], y_dn))
-
-    def y_last(s):
-        for copy in y1[s][2:] + y2[s]:
-            copy.wait_recv()
-        ysum[s, 0:2] = (pb[s, y, A].astype(F32) + yin[s, 3].astype(F32)
-                        + yin[s, 4].astype(F32)).astype(BF16).reshape(2, 192, 128)
-        ysum[s, 2:4] = (pb[s, y, B].astype(F32) + yin[s, 2].astype(F32)
-                        + yin[s, 5].astype(F32)).astype(BF16).reshape(2, 192, 128)
-        xs[s] = [send(ysum.at[s, up(x, d)], xin.at[s, x], at(dx=d)) for d in (2, 1, -1)]
-        xin[s, x] = ysum[s, x]
-
-    def z_first(s):
-        for copy in xs[s]:
-            copy.wait_recv()
-        z1[s] = (send(xin.at[s, ho, TA], zin.at[s, 0], z_up),
-                 send(xin.at[s, ho, TB], zin.at[s, 1], z_dn),
-                 send(xin.at[s, hr, TB], zin.at[s, 2], z_up),
-                 send(xin.at[s, hl, TA], zin.at[s, 3], z_dn))
-
-    def z_second(s):
-        z1[s][0].wait_recv()
-        zbuf[s, 0] = (xin[s, hr, TA].astype(F32) + zin[s, 0].astype(F32)).astype(BF16)
-        up_copy = send(zbuf.at[s, 0], zin.at[s, 4], z_up)
-        z1[s][1].wait_recv()
-        zbuf[s, 1] = (xin[s, hl, TB].astype(F32) + zin[s, 1].astype(F32)).astype(BF16)
-        z2[s] = (up_copy, send(zbuf.at[s, 1], zin.at[s, 5], z_dn))
-
-    def z_last(s):
-        for copy in z1[s][2:] + z2[s]:
-            copy.wait_recv()
-        top = xin[s, zh, TA].astype(F32) + zin[s, 3].astype(F32) + zin[s, 4].astype(F32)
-        bot = xin[s, zh, TB].astype(F32) + zin[s, 2].astype(F32) + zin[s, 5].astype(F32)
-        for rows, v in ((slice(0, 96), top), (slice(96, 192), bot)):
-            out_ref[rows, 64 * s:64 * s + 64] = v[:, 0:64]
-            out_ref[rows, 192 + 64 * s:192 + 64 * s + 64] = v[:, 64:128]
-
-    columns_in(0)
-    r_et.wait_recv()
-    r_wb.wait_recv()
-    product(0)
-    y_first(0)
-    columns_in(1)
-    product(1)
-    y_second(0)
-    y_first(1)
-    columns_in(2)
-    product(2)
-    y_second(1)
-    y_first(2)
-    y_last(0)
-    y_second(2)
-    z_first(0)
-    y_last(1)
-    z_second(0)
-    z_first(1)
-    y_last(2)
-    z_second(1)
-    z_last(0)
-    z_first(2)
-    z_last(1)
-    z_second(2)
-    z_last(2)
+                for t in range(2):
+                    for j in range(2):
+                        pb[2 * s + t, 2 * half + j, 96 * bx:96 * bx + 96] = (
+                            p[96 * t:96 * t + 96, 128 * j:128 * j + 128])
+
+    def y_first(k):
+        if k % 2 == 0:
+            columns_in(k // 2)
+            if k == 0:
+                for copy in (r_e2, r_w2, r_et, r_wb):
+                    copy.wait_recv()
+            product(k // 2)
+        y1[k] = (send(pb.at[k, yo, A], yin.at[k, 0], y_up),
+                 send(pb.at[k, yo, B], yin.at[k, 1], y_dn),
+                 send(pb.at[k, yr, B], yin.at[k, 2], y_up),
+                 send(pb.at[k, yl, A], yin.at[k, 3], y_dn))
+
+    def y_second(k):
+        y1[k][0].wait_recv()
+        pb[k, yr, A] = (pb[k, yr, A].astype(F32) + yin[k, 0].astype(F32)).astype(BF16)
+        up_copy = send(pb.at[k, yr, A], yin.at[k, 4], y_up)
+        y1[k][1].wait_recv()
+        pb[k, yl, B] = (pb[k, yl, B].astype(F32) + yin[k, 1].astype(F32)).astype(BF16)
+        y2[k] = (up_copy, send(pb.at[k, yl, B], yin.at[k, 5], y_dn))
+
+    def y_last(k):
+        for copy in y1[k][2:] + y2[k]:
+            copy.wait_recv()
+        ysum[k, 0:2] = (pb[k, y, A].astype(F32) + yin[k, 3].astype(F32)
+                        + yin[k, 4].astype(F32)).astype(BF16).reshape(2, 96, 128)
+        ysum[k, 2:4] = (pb[k, y, B].astype(F32) + yin[k, 2].astype(F32)
+                        + yin[k, 5].astype(F32)).astype(BF16).reshape(2, 96, 128)
+        xs[k] = [send(ysum.at[k, up(x, d)], xin.at[k, x], at(dx=d)) for d in (2, 1, -1)]
+        xin[k, x] = ysum[k, x]
+
+    def z_first(k):
+        for copy in xs[k]:
+            copy.wait_recv()
+        z1[k] = (send(xin.at[k, ho, TA], zin.at[k, 0], z_up),
+                 send(xin.at[k, ho, TB], zin.at[k, 1], z_dn),
+                 send(xin.at[k, hr, TB], zin.at[k, 2], z_up),
+                 send(xin.at[k, hl, TA], zin.at[k, 3], z_dn))
+
+    def z_second(k):
+        z1[k][0].wait_recv()
+        zbuf[k, 0] = (xin[k, hr, TA].astype(F32) + zin[k, 0].astype(F32)).astype(BF16)
+        up_copy = send(zbuf.at[k, 0], zin.at[k, 4], z_up)
+        z1[k][1].wait_recv()
+        zbuf[k, 1] = (xin[k, hl, TB].astype(F32) + zin[k, 1].astype(F32)).astype(BF16)
+        z2[k] = (up_copy, send(zbuf.at[k, 1], zin.at[k, 5], z_dn))
+
+    def z_last(k):
+        for copy in z1[k][2:] + z2[k]:
+            copy.wait_recv()
+        top = xin[k, zh, TA].astype(F32) + zin[k, 3].astype(F32) + zin[k, 4].astype(F32)
+        bot = xin[k, zh, TB].astype(F32) + zin[k, 2].astype(F32) + zin[k, 5].astype(F32)
+        s, t = k // 2, k % 2
+        for first, v in ((96 * t, top), (96 * t + 48, bot)):
+            out_ref[first:first + 48, 64 * s:64 * s + 64] = v[:, 0:64]
+            out_ref[first:first + 48, 192 + 64 * s:192 + 64 * s + 64] = v[:, 64:128]
+
+    steps = ((z_last, 7), (z_second, 5), (z_first, 3), (y_last, 2), (y_second, 1), (y_first, 0))
+    for i in range(6 + 7):
+        for step, lag in steps:
+            if 0 <= i - lag < 6:
+                step(i - lag)
     for copy in copies:
         copy.wait_send()
 
@@ -286,7 +277,7 @@
     return pl.pallas_call(
         kernel,
         out_shape=jax.ShapeDtypeStruct((192, 384), F32),
-        in_specs=[pl.BlockSpec(memory_space=pl.ANY)] * 2,
+        in_specs=[pl.BlockSpec(memory_space=pltpu.HBM)] * 2,
         out_specs=pl.BlockSpec(memory_space=pltpu.VMEM),
         scratch_shapes=[
             pltpu.VMEM((4, 4, 2, 192, 512), BF16),
@@ -294,12 +285,12 @@
             pltpu.VMEM((192, 512), F32),
             pltpu.VMEM((4, 192, 512), BF16),
             pltpu.VMEM((3, 4, 2, 64, 512), BF16),
-            pltpu.VMEM((3, 4, 768, 128), BF16),
-            pltpu.VMEM((3, 6, 384, 128), BF16),
-            pltpu.VMEM((3, 4, 192, 128), BF16),
-            pltpu.VMEM((3, 4, 192, 128), BF16),
-            pltpu.VMEM((3, 6, 96, 128), BF16),
-            pltpu.VMEM((3, 2, 96, 128), BF16),
+            pltpu.VMEM((6, 4, 384, 128), BF16),
+            pltpu.VMEM((6, 6, 192, 128), BF16),
+            pltpu.VMEM((6, 4, 96, 128), BF16),
+            pltpu.VMEM((6, 4, 96, 128), BF16),
+            pltpu.VMEM((6, 6, 48, 128), BF16),
+            pltpu.VMEM((6, 2, 48, 128), BF16),
             pltpu.SemaphoreType.DMA((N_SEM,)),
             pltpu.SemaphoreType.DMA((N_SEM,)),
             pltpu.SemaphoreType.DMA((2,)),

time: 104 us -> 99.3 us (0.955)
  the two profiles are of different devices: /device:TPU:24 before, /device:TPU:1 now
where the time goes in v3:
time: 99.3 us; the launch traced here: 98.1 us
  Pallas kernels  94.8 us (95%)
  local copies, waits for them, and re-layouts  3.31 us (3%)
    pallas_call x1, Pallas kernels, local(): pl.pallas_call(kernel, out_shape=jax.ShapeDtypeStruct((192, 384), F32), i...  94.8 us
    unnamed x5, local copies, waits for them, and re-layouts  3.31 us

profile of v3, /device:TPU:1, one launch (start us, length us, event | category | flops | bytes accessed | tf_op | source)
XLA Modules:
  0.0 98.1 jit_solution(2957695564160596375)
XLA Ops:
  0.0 0.0 copy-start
  0.0 1.7 %copy-done = bf16[1,192,6144]{2,1,0:T(8,128)(2,1)S(1)} copy-done((bf16[1,192,6144]{2,1,0:T(8,128)(2,1)S(1)}, bf16[1,192,6144]{2,1,0:T(8,128)(2,1)}, u32[]{:S(2)}) %copy-start) | copy-done | bytes 2359320
  1.7 0.0 copy-start.1
  1.7 0.9 copy-done.1
  2.6 94.8 %exchange.1 = f32[192,384]{1,0:T(8,128)S(1)} custom-call(bf16[192,6144]{1,0:T(8,128)(2,1)S(1)} %bitcast.1, bf16[192,512]{1,0:T(8,128)(2,1)S(1)} %copy-done.1), custom_call_target="tpu_custom_call" | custom-call | tf_op jit(solution)/shard_map/exchange/pallas_call | solution.py:277
  97.4 0.7 copy.4
Async XLA Ops:
  0.0 1.7 %copy-start = (bf16[1,192,6144]{2,1,0:T(8,128)(2,1)S(1)}, bf16[1,192,6144]{2,1,0:T(8,128)(2,1)}, u32[]{:S(2)}) copy-start(bf16[1,192,6144]{2,1,0:T(8,128)(2,1)} %param.2) | copy-start | bytes 7077892
  1.7 0.9 copy-start.1

commit v4 on v3

--- a/solution.py
+++ b/solution.py
@@ -172,15 +172,16 @@
     def columns_out(s):
         return [same(hcol.at[s, zl, c], in_group(d)) for d in (1, 3, 2)]
 
-    r_e, r_w = same(hrow.at[x, TOP], east), same(hrow.at[x, BOT], west)
+    Q = [pl.ds(48 * j, 48) for j in range(4)]
+    r_in = [[same(hrow.at[x, TOP], east), same(hrow.at[x, TOP], west)]]
     c_in = [columns_out(0)]
-    r_e2, r_w2 = same(hrow.at[x, BOT], east), same(hrow.at[x, TOP], west)
+    r_in.append([same(hrow.at[x, BOT], east), same(hrow.at[x, BOT], west)])
     c_in += [columns_out(1), columns_out(2)]
     c_sib = [[same(hcol.at[s, zl, c], sibling)] for s in range(3)]
-    r_e.wait_recv()
-    r_et = same(hrow.at[xl, TOP], east)
-    r_w.wait_recv()
-    r_wb = same(hrow.at[xr, BOT], west)
+    for t in range(2):
+        for copy in r_in[t]:
+            copy.wait_recv()
+        r_in[t] = [same(hrow.at[xl, Q[2 * t]], east), same(hrow.at[xr, Q[2 * t + 1]], west)]
 
     yr, yl, yo = up(y, 1), up(y, -1), up(y, 2)
     y_up, y_dn = at(dy=1), at(dy=-1)
@@ -197,24 +198,23 @@
         for copy in c_sib[s]:
             copy.wait_recv()
 
-    def product(s):
+    def product(k):
+        s, t = k // 2, k % 2
+        rows = hrow[:, 96 * t:96 * t + 96].reshape(384, 512)
         for half in range(2):
             cols = hcol[s, 2 * half:2 * half + 2].reshape(256, 512)
-            for bx in range(4):
-                p = lax.dot_general(hrow[bx], cols, (((1,), (1,)), ((), ())), preferred_element_type=F32)
-                p = p.astype(BF16)
-                for t in range(2):
-                    for j in range(2):
-                        pb[2 * s + t, 2 * half + j, 96 * bx:96 * bx + 96] = (
-                            p[96 * t:96 * t + 96, 128 * j:128 * j + 128])
+            p = lax.dot_general(rows, cols, (((1,), (1,)), ((), ())), preferred_element_type=F32)
+            p = p.astype(BF16)
+            pb[k, 2 * half] = p[:, 0:128]
+            pb[k, 2 * half + 1] = p[:, 128:256]
 
     def y_first(k):
         if k % 2 == 0:
             columns_in(k // 2)
-            if k == 0:
-                for copy in (r_e2, r_w2, r_et, r_wb):
-                    copy.wait_recv()
-            product(k // 2)
+        if k < 2:
+            for copy in r_in[k]:
+                copy.wait_recv()
+        product(k)
         y1[k] = (send(pb.at[k, yo, A], yin.at[k, 0], y_up),
                  send(pb.at[k, yo, B], yin.at[k, 1], y_dn),
                  send(pb.at[k, yr, B], yin.at[k, 2], y_up),
@@ -264,11 +264,11 @@
             out_ref[first:first + 48, 64 * s:64 * s + 64] = v[:, 0:64]
             out_ref[first:first + 48, 192 + 64 * s:192 + 64 * s + 64] = v[:, 64:128]
 
-    steps = ((z_last, 7), (z_second, 5), (z_first, 3), (y_last, 2), (y_second, 1), (y_first, 0))
-    for i in range(6 + 7):
-        for step, lag in steps:
-            if 0 <= i - lag < 6:
-                step(i - lag)
+    steps = {"F": y_first, "S": y_second, "L": y_last, "f": z_first, "s": z_second, "l": z_last}
+    for part in ("F0F1S0F2S1F3L0S2F4", "L1S3F5f0L2f1S4L3S5f2s0L4s1f3L5",
+                 "s2l0f4f5s3l1s4l2s5l3l4l5"):
+        for j in range(0, len(part), 2):
+            steps[part[j]](int(part[j + 1]))
     for copy in copies:
         copy.wait_send()
 
@@ -296,7 +296,7 @@
             pltpu.SemaphoreType.DMA((2,)),
         ],
         compiler_params=pltpu.CompilerParams(
-            collective_id=0, has_side_effects=True, vmem_limit_bytes=48 << 20),
+            collective_id=0, has_side_effects=True, vmem_limit_bytes=60 << 20),
         name="exchange",
     )(integrals.reshape(192, 6144), occupied)
 

time: 99.3 us -> 94.7 us (0.954)
  Pallas kernels: 94.8 us -> 92.8 us
  local copies, waits for them, and re-layouts: 3.31 us -> 1.69 us
    pallas_call x1, Pallas kernels: 94.8 us -> 92.8 us  [local(): pl.pallas_call(kernel, out_shape=jax.ShapeDtypeStruct((192, 384), F32), i...]
    unnamed x5 -> x1, local copies, waits for them, and re-layouts: 3.31 us -> 1.69 us
where the time goes in v4:
time: 94.7 us; the launch traced here: 94.5 us
  Pallas kernels  92.8 us (98%)
  local copies, waits for them, and re-layouts  1.69 us (2%)
    pallas_call x1, Pallas kernels, local(): pl.pallas_call(kernel, out_shape=jax.ShapeDtypeStruct((192, 384), F32), i...  92.8 us

profile of v4, /device:TPU:1, one launch (start us, length us, event | category | flops | bytes accessed | tf_op | source)
XLA Modules:
  0.0 94.5 jit_solution(11679095300408365351)
XLA Ops:
  0.0 92.8 %exchange.1 = f32[192,384]{1,0:T(8,128)} custom-call(bf16[192,6144]{1,0:T(8,128)(2,1)} %bitcast.1, bf16[192,512]{1,0:T(8,128)(2,1)} %occ_hbm.1), custom_call_target="tpu_custom_call" | custom-call | tf_op jit(solution)/shard_map/exchange/pallas_call | solution.py:277
  92.8 1.7 %copy.4 = f32[192,384]{1,0:T(8,128)} copy(f32[192,384]{1,0:T(8,128)} %exchange.1) | data formatting | bytes 589824

commit v5 on v4

--- a/solution.py
+++ b/solution.py
@@ -9,7 +9,7 @@
 F32 = jnp.float32
 BF16 = jnp.bfloat16
 
-N_SEM = 192
+N_SEM = 288
 
 
 def kernel(ints_hbm, occ_hbm, out_ref, occ, ints, hacc, hrow, hcol, pb,
@@ -61,15 +61,29 @@
     xr, xl, xo = up(x, 1), up(x, -1), up(x, 2)
     zr, zd, zo = up(zl, 1), up(zl, -1), up(zl, 2)
     east, west, north, south = at(dx=1), at(dx=-1), at(dz=1), at(dz=-1)
+    y_up, y_dn = at(dy=1), at(dy=-1)
     PA, PB = pl.ds(0, 256), pl.ds(256, 256)
-    ALL, TOP, BOT = pl.ds(0, 192), pl.ds(0, 96), pl.ds(96, 96)
+    odd = y % 2
+
+    def rows_at(first, step, size):
+        return pl.ds(pl.multiple_of(first + step * odd, 32), size)
+
+    GOT, TOP, BOT = rows_at(0, 64, 128), rows_at(0, 64, 64), rows_at(64, 64, 64)
+    UP, DOWN, LACK = rows_at(0, 160, 32), rows_at(32, 96, 32), rows_at(128, -128, 64)
 
     def blk(bz, bx, rows, cols):
         return occ.at[bz, bx, c, rows, cols]
 
+    def over_y(bz, bx, cols):
+        return [same(blk(bz, bx, UP, cols), y_up), same(blk(bz, bx, DOWN, cols), y_dn)]
+
+    def landed(group):
+        for copy in group:
+            copy.wait_recv()
+
     fwd_a = [[], []]
     fwd_b = [[], []]
-    own_a, own_b = blk(zl, x, ALL, PA), blk(zl, x, ALL, PB)
+    own_a, own_b = blk(zl, x, GOT, PA), blk(zl, x, GOT, PB)
     a_e, a_w = same(own_a, east), same(own_a, west)
     b_n, b_s = same(own_b, north), same(own_b, south)
     fwd_a[0].append(same(own_a, north))
@@ -80,50 +94,54 @@
 
     a_e.wait_recv()
     a_et = same(blk(zl, xl, TOP, PA), east)
-    fwd_a[0].append(same(blk(zl, xl, ALL, PA), north))
-    fwd_a[1].append(same(blk(zl, xl, ALL, PA), south))
+    fwd_a[0].append(same(blk(zl, xl, GOT, PA), north))
+    fwd_a[1].append(same(blk(zl, xl, GOT, PA), south))
     b_n.wait_recv()
     b_nt = same(blk(zd, x, TOP, PB), north)
-    fwd_b[0].append(same(blk(zd, x, ALL, PB), east))
-    fwd_b[1].append(same(blk(zd, x, ALL, PB), west))
+    fwd_b[0].append(same(blk(zd, x, GOT, PB), east))
+    fwd_b[1].append(same(blk(zd, x, GOT, PB), west))
+    y_a0, y_b0 = [over_y(zl, xl, PA)], [over_y(zd, x, PB)]
     a_w.wait_recv()
     a_wb = same(blk(zl, xr, BOT, PA), west)
-    fwd_a[0].append(same(blk(zl, xr, ALL, PA), north))
-    fwd_a[1].append(same(blk(zl, xr, ALL, PA), south))
+    fwd_a[0].append(same(blk(zl, xr, GOT, PA), north))
+    fwd_a[1].append(same(blk(zl, xr, GOT, PA), south))
     b_s.wait_recv()
     b_sb = same(blk(zr, x, BOT, PB), south)
-    fwd_b[0].append(same(blk(zr, x, ALL, PB), east))
-    fwd_b[1].append(same(blk(zr, x, ALL, PB), west))
-    sib_a0 = [sib_own, same(blk(zl, xl, ALL, PA), sibling), same(blk(zl, xr, ALL, PA), sibling)]
-    sib_b0 = [same(blk(zd, x, ALL, PB), sibling), same(blk(zr, x, ALL, PB), sibling)]
-    a_et.wait_recv()
-    a_wb.wait_recv()
-    fwd_a[0].append(same(blk(zl, xo, ALL, PA), north))
-    fwd_a[1].append(same(blk(zl, xo, ALL, PA), south))
-    sib_a0.append(same(blk(zl, xo, ALL, PA), sibling))
-    b_nt.wait_recv()
-    b_sb.wait_recv()
-    fwd_b[0].append(same(blk(zo, x, ALL, PB), east))
-    fwd_b[1].append(same(blk(zo, x, ALL, PB), west))
-    sib_b0.append(same(blk(zo, x, ALL, PB), sibling))
-
-    last_a, last_b = [], []
-    sib_a1, sib_b1 = [], []
+    fwd_b[0].append(same(blk(zr, x, GOT, PB), east))
+    fwd_b[1].append(same(blk(zr, x, GOT, PB), west))
+    y_a0.append(over_y(zl, xr, PA))
+    y_b0.append(over_y(zr, x, PB))
+    sib_0 = [sib_own, same(blk(zl, xl, GOT, PA), sibling), same(blk(zl, xr, GOT, PA), sibling),
+             same(blk(zd, x, GOT, PB), sibling), same(blk(zr, x, GOT, PB), sibling)]
+    landed((a_et, a_wb))
+    fwd_a[0].append(same(blk(zl, xo, GOT, PA), north))
+    fwd_a[1].append(same(blk(zl, xo, GOT, PA), south))
+    y_a0.append(over_y(zl, xo, PA))
+    landed((b_nt, b_sb))
+    fwd_b[0].append(same(blk(zo, x, GOT, PB), east))
+    fwd_b[1].append(same(blk(zo, x, GOT, PB), west))
+    y_b0.append(over_y(zo, x, PB))
+    sib_0 += [same(blk(zl, xo, GOT, PA), sibling), same(blk(zo, x, GOT, PB), sibling)]
+
+    last = []
+    sib_1 = []
+    y_1 = [[], [], [], []]
     for bx, bz, j in zip((x, xl, xr, xo), (zl, zd, zr, zo), range(4)):
         fwd_a[0][j].wait_recv()
         t = same(blk(zd, bx, TOP, PA), north)
-        sib_a1.append(same(blk(zd, bx, ALL, PA), sibling))
         fwd_a[1][j].wait_recv()
         u = same(blk(zr, bx, BOT, PA), south)
-        sib_a1.append(same(blk(zr, bx, ALL, PA), sibling))
-        last_a.append((t, u, bx))
         fwd_b[0][j].wait_recv()
-        t = same(blk(bz, xl, TOP, PB), east)
-        sib_b1.append(same(blk(bz, xl, ALL, PB), sibling))
+        v = same(blk(bz, xl, TOP, PB), east)
         fwd_b[1][j].wait_recv()
-        u = same(blk(bz, xr, BOT, PB), west)
-        sib_b1.append(same(blk(bz, xr, ALL, PB), sibling))
-        last_b.append((t, u, bz))
+        w = same(blk(bz, xr, BOT, PB), west)
+        last.append((t, u, v, w))
+        y_1[0] += over_y(zd, bx, PA)
+        y_1[1] += over_y(zr, bx, PA)
+        y_1[2] += over_y(bz, xl, PB)
+        y_1[3] += over_y(bz, xr, PB)
+        sib_1 += [same(blk(zd, bx, GOT, PA), sibling), same(blk(zr, bx, GOT, PA), sibling),
+                  same(blk(bz, xl, GOT, PB), sibling), same(blk(bz, xr, GOT, PB), sibling)]
 
     def lanes(start, size):
         return pl.ds(pl.multiple_of(start, 128), size)
@@ -140,27 +158,40 @@
             total = term if total is None else total + term
         return total
 
+    def final_hop(j, bx, bz):
+        t, u, v, w = last[j]
+        landed((t, u))
+        y_2[0] += over_y(zo, bx, PA)
+        landed((v, w))
+        y_2[1] += over_y(bz, xo, PB)
+        sib_2.append(same(blk(zo, bx, GOT, PA), sibling))
+        sib_2.append(same(blk(bz, xo, GOT, PB), sibling))
+
+    sib_2, y_2 = [], [[], []]
+    for bx, bz, group_a, group_b in zip((xl, xr, xo), (zd, zr, zo), y_a0, y_b0):
+        landed(group_a + group_b)
+        sib_0 += [same(blk(zl, bx, LACK, PA), sibling), same(blk(bz, x, LACK, PB), sibling)]
+    final_hop(0, x, zl)
     ints_copy.wait()
-    for copy in sib_a0 + sib_b0:
-        copy.wait_recv()
+    landed(sib_0)
     hacc[:, 0:256] = part_a(zl)
     hacc[:, 256:512] = part_b(x)
-    for copy in sib_a1 + sib_b1:
-        copy.wait_recv()
+    final_hop(1, xl, zd)
+    for bz, bx, group_a, group_b in ((zd, xl, y_1[0], y_1[2]), (zr, xr, y_1[1], y_1[3])):
+        landed(group_a + group_b)
+        sib_1 += [same(occ.at[bz, :, c, LACK, PA], sibling), same(occ.at[:, bx, c, LACK, PB], sibling)]
+    final_hop(2, xr, zr)
+    final_hop(3, xo, zo)
+    landed(sib_1)
     hacc[:, 0:256] += part_a(zd)
     hacc[:, 256:512] += part_b(xl)
     hacc[:, 0:256] += part_a(zr)
     hacc[:, 256:512] += part_b(xr)
-    sib_2 = []
-    for (t, u, bx), (v, w, bz) in zip(last_a, last_b):
-        t.wait_recv()
-        u.wait_recv()
-        sib_2.append(same(blk(zo, bx, ALL, PA), sibling))
-        v.wait_recv()
-        w.wait_recv()
-        sib_2.append(same(blk(bz, xo, ALL, PB), sibling))
-    for copy in sib_2:
-        copy.wait_recv()
+    landed(y_2[0])
+    sib_2.append(same(occ.at[zo, :, c, LACK, PA], sibling))
+    landed(y_2[1])
+    sib_2.append(same(occ.at[:, xo, c, LACK, PB], sibling))
+    landed(sib_2)
     h_a = (hacc[:, 0:256] + part_a(zo)).astype(BF16)
     h_b = (hacc[:, 256:512] + part_b(xo)).astype(BF16)
     hrow[x, :, 0:256] = h_a
@@ -172,10 +203,11 @@
     def columns_out(s):
         return [same(hcol.at[s, zl, c], in_group(d)) for d in (1, 3, 2)]
 
+    UPPER, LOWER = pl.ds(0, 96), pl.ds(96, 96)
     Q = [pl.ds(48 * j, 48) for j in range(4)]
-    r_in = [[same(hrow.at[x, TOP], east), same(hrow.at[x, TOP], west)]]
+    r_in = [[same(hrow.at[x, UPPER], east), same(hrow.at[x, UPPER], west)]]
     c_in = [columns_out(0)]
-    r_in.append([same(hrow.at[x, BOT], east), same(hrow.at[x, BOT], west)])
+    r_in.append([same(hrow.at[x, LOWER], east), same(hrow.at[x, LOWER], west)])
     c_in += [columns_out(1), columns_out(2)]
     c_sib = [[same(hcol.at[s, zl, c], sibling)] for s in range(3)]
     for t in range(2):
@@ -184,7 +216,6 @@
         r_in[t] = [same(hrow.at[xl, Q[2 * t]], east), same(hrow.at[xr, Q[2 * t + 1]], west)]
 
     yr, yl, yo = up(y, 1), up(y, -1), up(y, 2)
-    y_up, y_dn = at(dy=1), at(dy=-1)
     hr, hl, ho = up(zh, 1), up(zh, -1), up(zh, 2)
     z_up, z_dn = at(dz=4), at(dz=-4)
     A, B = pl.ds(0, 192), pl.ds(192, 192)

time: 94.7 us -> 97.2 us (1.026)
  Pallas kernels: 92.8 us -> 94.9 us
    pallas_call x1, Pallas kernels: 92.8 us -> 94.9 us  [local(): pl.pallas_call(kernel, out_shape=jax.ShapeDtypeStruct((192, 384), F32), i...]
where the time goes in v5:
time: 97.2 us; the launch traced here: 96.6 us
  Pallas kernels  94.9 us (98%)
  local copies, waits for them, and re-layouts  1.69 us (2%)
    pallas_call x1, Pallas kernels, local(): pl.pallas_call(kernel, out_shape=jax.ShapeDtypeStruct((192, 384), F32), i...  94.9 us

profile of v5, /device:TPU:1, one launch (start us, length us, event | category | flops | bytes accessed | tf_op | source)
XLA Modules:
  0.0 96.6 jit_solution(5620243595364369419)
XLA Ops:
  0.0 94.9 %exchange.1 = f32[192,384]{1,0:T(8,128)} custom-call(bf16[192,6144]{1,0:T(8,128)(2,1)} %bitcast.1, bf16[192,512]{1,0:T(8,128)(2,1)} %occ_hbm.1), custom_call_target="tpu_custom_call" | custom-call | tf_op jit(solution)/shard_map/exchange/pallas_call | solution.py:308
  94.9 1.7 %copy.4 = f32[192,384]{1,0:T(8,128)} copy(f32[192,384]{1,0:T(8,128)} %exchange.1) | data formatting | bytes 589824

commit v6 on v4

v6 whole, which is shorter than its diff:
```python
import jax
import jax.numpy as jnp
from jax import lax
from jax.experimental import pallas as pl
from jax.experimental.pallas import tpu as pltpu
from jax.sharding import PartitionSpec as P

MESH = pl.DeviceIdType.MESH
F32 = jnp.float32
BF16 = jnp.bfloat16

N_SEM = 73


def kernel(ints_hbm, occ_hbm, out_ref, occ, ints, hacc, hrow, hcol, pb,
           yin, ysum, xin, zin, zbuf, ssem, rsem, lsem):
    grp, row = lax.axis_index("grp"), lax.axis_index("row")
    y, zh = grp // 4, grp % 4
    zl, x, c = row // 8, (row // 2) % 4, row % 2
    z = zh * 4 + zl

    def up(v, d, n=4):
        return (v + d + n) % n

    def at(dx=0, dy=0, dz=0):
        zz = up(z, dz, 16)
        return (up(y, dy) * 4 + zz // 4, (zz % 4) * 8 + up(x, dx) * 2 + c)

    def in_group(d):
        return (grp, up(zl, d) * 8 + x * 2 + c)

    sibling = (grp, zl * 8 + x * 2 + (1 - c))

    made = [0]

    def arrival():
        made[0] += 1
        return made[0] - 1

    def send(src, dst, to, sem, group):
        pltpu.make_async_remote_copy(
            src_ref=src, dst_ref=dst, send_sem=ssem.at[group], recv_sem=rsem.at[sem],
            device_id=to, device_id_type=MESH).start()
        return sem

    def same(ref, to, sem, group):
        return send(ref, ref, to, sem, group)

    def waiting(ref, sem, group):
        return pltpu.make_async_remote_copy(
            src_ref=ref, dst_ref=ref, send_sem=ssem.at[group], recv_sem=rsem.at[sem],
            device_id=sibling, device_id_type=MESH)

    def landed(sem, ref):
        waiting(ref, sem, 0).wait_recv()

    own_copy = pltpu.make_async_copy(occ_hbm, occ.at[zl, x, c], lsem.at[0])
    own_copy.start()
    ints_copy = pltpu.make_async_copy(ints_hbm, ints, lsem.at[1])
    ints_copy.start()

    barrier = pltpu.get_barrier_semaphore()
    partners = [sibling, at(dx=1), at(dx=2), at(dx=-1), at(dy=1), at(dy=-1), at(dz=1), at(dz=-1),
                at(dz=4), at(dz=-4), in_group(1), in_group(2), in_group(3)]
    for partner in partners:
        pl.semaphore_signal(barrier, inc=1, device_id=partner, device_id_type=MESH)
    pl.semaphore_wait(barrier, len(partners))
    own_copy.wait()

    xr, xl, xo = up(x, 1), up(x, -1), up(x, 2)
    zr, zd, zo = up(zl, 1), up(zl, -1), up(zl, 2)
    east, west, north, south = at(dx=1), at(dx=-1), at(dz=1), at(dz=-1)
    PA, PB = pl.ds(0, 256), pl.ds(256, 256)
    ALL, TOP, BOT = pl.ds(0, 192), pl.ds(0, 96), pl.ds(96, 96)

    def blk(bz, bx, rows, cols):
        return occ.at[bz, bx, c, rows, cols]

    GATHER, SIBLING, BLOCKS, SUMS = range(4)
    half_block = blk(zl, x, ALL, PA)

    def hop(ref, to, sem=None):
        return same(ref, to, arrival() if sem is None else sem, GATHER)

    def over(ref, sem):
        return same(ref, sibling, sem, SIBLING)

    sib_0, sib_1, sib_2 = arrival(), arrival(), arrival()
    fwd_a = [[], []]
    fwd_b = [[], []]
    own_a, own_b = blk(zl, x, ALL, PA), blk(zl, x, ALL, PB)
    a_e, a_w = hop(own_a, east), hop(own_a, west)
    b_n, b_s = hop(own_b, north), hop(own_b, south)
    fwd_a[0].append(hop(own_a, north))
    fwd_a[1].append(hop(own_a, south))
    fwd_b[0].append(hop(own_b, east))
    fwd_b[1].append(hop(own_b, west))
    over(occ.at[zl, x, c], sib_0)

    a_2, b_2 = arrival(), arrival()
    landed(a_e, half_block)
    hop(blk(zl, xl, TOP, PA), east, a_2)
    fwd_a[0].append(hop(blk(zl, xl, ALL, PA), north))
    fwd_a[1].append(hop(blk(zl, xl, ALL, PA), south))
    landed(b_n, half_block)
    hop(blk(zd, x, TOP, PB), north, b_2)
    fwd_b[0].append(hop(blk(zd, x, ALL, PB), east))
    fwd_b[1].append(hop(blk(zd, x, ALL, PB), west))
    landed(a_w, half_block)
    hop(blk(zl, xr, BOT, PA), west, a_2)
    fwd_a[0].append(hop(blk(zl, xr, ALL, PA), north))
    fwd_a[1].append(hop(blk(zl, xr, ALL, PA), south))
    landed(b_s, half_block)
    hop(blk(zr, x, BOT, PB), south, b_2)
    fwd_b[0].append(hop(blk(zr, x, ALL, PB), east))
    fwd_b[1].append(hop(blk(zr, x, ALL, PB), west))
    over(blk(zl, xl, ALL, PA), sib_0)
    over(blk(zl, xr, ALL, PA), sib_0)
    over(blk(zd, x, ALL, PB), sib_0)
    over(blk(zr, x, ALL, PB), sib_0)
    landed(a_2, half_block)
    fwd_a[0].append(hop(blk(zl, xo, ALL, PA), north))
    fwd_a[1].append(hop(blk(zl, xo, ALL, PA), south))
    over(blk(zl, xo, ALL, PA), sib_0)
    landed(b_2, half_block)
    fwd_b[0].append(hop(blk(zo, x, ALL, PB), east))
    fwd_b[1].append(hop(blk(zo, x, ALL, PB), west))
    over(blk(zo, x, ALL, PB), sib_0)

    last = []
    for bx, bz, j in zip((x, xl, xr, xo), (zl, zd, zr, zo), range(4)):
        last_a, last_b = arrival(), arrival()
        landed(fwd_a[0][j], half_block)
        hop(blk(zd, bx, TOP, PA), north, last_a)
        over(blk(zd, bx, ALL, PA), sib_1)
        landed(fwd_a[1][j], half_block)
        hop(blk(zr, bx, BOT, PA), south, last_a)
        over(blk(zr, bx, ALL, PA), sib_1)
        landed(fwd_b[0][j], half_block)
        hop(blk(bz, xl, TOP, PB), east, last_b)
        over(blk(bz, xl, ALL, PB), sib_1)
        landed(fwd_b[1][j], half_block)
        hop(blk(bz, xr, BOT, PB), west, last_b)
        over(blk(bz, xr, ALL, PB), sib_1)
        last.append((last_a, bx, last_b, bz))

    def lanes(start, size):
        return pl.ds(pl.multiple_of(start, 128), size)

    def part_a(bz):
        return jnp.dot(ints[:, lanes(bz * 1536, 1536)],
                       occ[bz, :, :, :, 0:256].reshape(1536, 256), preferred_element_type=F32)

    def part_b(bx):
        total = None
        for bz in range(4):
            term = jnp.dot(ints[:, lanes(bz * 1536 + bx * 384, 384)],
                           occ[bz, bx, :, :, 256:512].reshape(384, 256), preferred_element_type=F32)
            total = term if total is None else total + term
        return total

    ints_copy.wait()
    landed(sib_0, occ.at[zl, :, 1 - c])
    hacc[:, 0:256] = part_a(zl)
    hacc[:, 256:512] = part_b(x)
    landed(sib_1, occ.at[zl])
    hacc[:, 0:256] += part_a(zd)
    hacc[:, 256:512] += part_b(xl)
    hacc[:, 0:256] += part_a(zr)
    hacc[:, 256:512] += part_b(xr)
    for last_a, bx, last_b, bz in last:
        landed(last_a, half_block)
        over(blk(zo, bx, ALL, PA), sib_2)
        landed(last_b, half_block)
        over(blk(bz, xo, ALL, PB), sib_2)
    landed(sib_2, occ.at[zl, :, 1 - c])
    h_a = (hacc[:, 0:256] + part_a(zo)).astype(BF16)
    h_b = (hacc[:, 256:512] + part_b(xo)).astype(BF16)
    hrow[x, :, 0:256] = h_a
    hrow[x, :, 256:512] = h_b
    for s in range(3):
        hcol[s, zl, c, :, 0:256] = h_a[64 * s:64 * s + 64]
        hcol[s, zl, c, :, 256:512] = h_b[64 * s:64 * s + 64]

    def columns_out(s):
        sem = arrival()
        for d in (1, 3, 2):
            same(hcol.at[s, zl, c], in_group(d), sem, BLOCKS)
        return sem

    Q = [pl.ds(48 * j, 48) for j in range(4)]
    r_1, r_2 = [arrival(), arrival()], [arrival(), arrival()]
    same(hrow.at[x, TOP], east, r_1[0], BLOCKS)
    same(hrow.at[x, TOP], west, r_1[0], BLOCKS)
    c_in = [columns_out(0)]
    same(hrow.at[x, BOT], east, r_1[1], BLOCKS)
    same(hrow.at[x, BOT], west, r_1[1], BLOCKS)
    c_in += [columns_out(1), columns_out(2)]
    c_sib = [arrival() for s in range(3)]
    for s in range(3):
        same(hcol.at[s, zl, c], sibling, c_sib[s], BLOCKS)
    for t in range(2):
        landed(r_1[t], hrow.at[x])
        same(hrow.at[xl, Q[2 * t]], east, r_2[t], BLOCKS)
        same(hrow.at[xr, Q[2 * t + 1]], west, r_2[t], BLOCKS)

    yr, yl, yo = up(y, 1), up(y, -1), up(y, 2)
    y_up, y_dn = at(dy=1), at(dy=-1)
    hr, hl, ho = up(zh, 1), up(zh, -1), up(zh, 2)
    z_up, z_dn = at(dz=4), at(dz=-4)
    A, B = pl.ds(0, 192), pl.ds(192, 192)
    TA, TB = pl.ds(0, 48), pl.ds(48, 48)
    y1, y2, xs, z1, z2 = {}, {}, {}, {}, {}

    def columns_in(s):
        landed(c_in[s], hcol.at[s, 0:3, c])
        for d in (1, 3, 2):
            same(hcol.at[s, up(zl, d), c], sibling, c_sib[s], BLOCKS)
        landed(c_sib[s], hcol.at[s, :, 1 - c])

    def product(k):
        s, t = k // 2, k % 2
        rows = hrow[:, 96 * t:96 * t + 96].reshape(384, 512)
        for half in range(2):
            cols = hcol[s, 2 * half:2 * half + 2].reshape(256, 512)
            p = lax.dot_general(rows, cols, (((1,), (1,)), ((), ())), preferred_element_type=F32)
            p = p.astype(BF16)
            pb[k, 2 * half] = p[:, 0:128]
            pb[k, 2 * half + 1] = p[:, 128:256]

    def pass_on(src, dst, to, sem):
        send(src, dst, to, sem, SUMS)

    def y_first(k):
        if k % 2 == 0:
            columns_in(k // 2)
        if k < 2:
            landed(r_2[k], hrow.at[x, TOP])
        product(k)
        y1[k], y2[k] = arrival(), arrival()
        pass_on(pb.at[k, yo, A], yin.at[k, 0], y_up, y1[k])
        pass_on(pb.at[k, yo, B], yin.at[k, 1], y_dn, y1[k])
        pass_on(pb.at[k, yr, B], yin.at[k, 2], y_up, y2[k])
        pass_on(pb.at[k, yl, A], yin.at[k, 3], y_dn, y2[k])

    def y_second(k):
        landed(y1[k], yin.at[k, 0:2])
        pb[k, yr, A] = (pb[k, yr, A].astype(F32) + yin[k, 0].astype(F32)).astype(BF16)
        pass_on(pb.at[k, yr, A], yin.at[k, 4], y_up, y2[k])
        pb[k, yl, B] = (pb[k, yl, B].astype(F32) + yin[k, 1].astype(F32)).astype(BF16)
        pass_on(pb.at[k, yl, B], yin.at[k, 5], y_dn, y2[k])

    def y_last(k):
        landed(y2[k], yin.at[k, 2:6])
        ysum[k, 0:2] = (pb[k, y, A].astype(F32) + yin[k, 3].astype(F32)
                        + yin[k, 4].astype(F32)).astype(BF16).reshape(2, 96, 128)
        ysum[k, 2:4] = (pb[k, y, B].astype(F32) + yin[k, 2].astype(F32)
                        + yin[k, 5].astype(F32)).astype(BF16).reshape(2, 96, 128)
        xs[k] = arrival()
        for d in (2, 1, -1):
            pass_on(ysum.at[k, up(x, d)], xin.at[k, x], at(dx=d), xs[k])
        xin[k, x] = ysum[k, x]

    def z_first(k):
        landed(xs[k], xin.at[k, 0:3])
        z1[k], z2[k] = arrival(), arrival()
        pass_on(xin.at[k, ho, TA], zin.at[k, 0], z_up, z1[k])
        pass_on(xin.at[k, ho, TB], zin.at[k, 1], z_dn, z1[k])
        pass_on(xin.at[k, hr, TB], zin.at[k, 2], z_up, z2[k])
        pass_on(xin.at[k, hl, TA], zin.at[k, 3], z_dn, z2[k])

    def z_second(k):
        landed(z1[k], zin.at[k, 0:2])
        zbuf[k, 0] = (xin[k, hr, TA].astype(F32) + zin[k, 0].astype(F32)).astype(BF16)
        pass_on(zbuf.at[k, 0], zin.at[k, 4], z_up, z2[k])
        zbuf[k, 1] = (xin[k, hl, TB].astype(F32) + zin[k, 1].astype(F32)).astype(BF16)
        pass_on(zbuf.at[k, 1], zin.at[k, 5], z_dn, z2[k])

    def z_last(k):
        landed(z2[k], zin.at[k, 2:6])
        top = xin[k, zh, TA].astype(F32) + zin[k, 3].astype(F32) + zin[k, 4].astype(F32)
        bot = xin[k, zh, TB].astype(F32) + zin[k, 2].astype(F32) + zin[k, 5].astype(F32)
        s, t = k // 2, k % 2
        for first, v in ((96 * t, top), (96 * t + 48, bot)):
            out_ref[first:first + 48, 64 * s:64 * s + 64] = v[:, 0:64]
            out_ref[first:first + 48, 192 + 64 * s:192 + 64 * s + 64] = v[:, 64:128]

    steps = {"F": y_first, "S": y_second, "L": y_last, "f": z_first, "s": z_second, "l": z_last}
    for part in ("F0F1S0F2S1F3L0S2F4", "L1S3F5f0L2f1S4L3S5f2s0L4s1f3L5",
                 "s2l0f4f5s3l1s4l2s5l3l4l5"):
        for j in range(0, len(part), 2):
            steps[part[j]](int(part[j + 1]))
    for group, ref in ((GATHER, occ.at[0:3, 0:3, :, 0:160]), (SIBLING, occ.at[:, :, 0]),
                       (BLOCKS, occ.at[0:3, :, 0, 0:160]), (SUMS, occ.at[0:3, 0:3, :, 0:144])):
        waiting(ref, 0, group).wait_send()
    assert made[0] == N_SEM, made[0]


def local(integrals, occupied):
    return pl.pallas_call(
        kernel,
        out_shape=jax.ShapeDtypeStruct((192, 384), F32),
        in_specs=[pl.BlockSpec(memory_space=pltpu.HBM)] * 2,
        out_specs=pl.BlockSpec(memory_space=pltpu.VMEM),
        scratch_shapes=[
            pltpu.VMEM((4, 4, 2, 192, 512), BF16),
            pltpu.VMEM((192, 6144), BF16),
            pltpu.VMEM((192, 512), F32),
            pltpu.VMEM((4, 192, 512), BF16),
            pltpu.VMEM((3, 4, 2, 64, 512), BF16),
            pltpu.VMEM((6, 4, 384, 128), BF16),
            pltpu.VMEM((6, 6, 192, 128), BF16),
            pltpu.VMEM((6, 4, 96, 128), BF16),
            pltpu.VMEM((6, 4, 96, 128), BF16),
            pltpu.VMEM((6, 6, 48, 128), BF16),
            pltpu.VMEM((6, 2, 48, 128), BF16),
            pltpu.SemaphoreType.DMA((4,)),
            pltpu.SemaphoreType.DMA((N_SEM,)),
            pltpu.SemaphoreType.DMA((2,)),
        ],
        compiler_params=pltpu.CompilerParams(
            collective_id=0, has_side_effects=True, vmem_limit_bytes=60 << 20),
        name="exchange",
    )(integrals.reshape(192, 6144), occupied)


def solution(mesh):
    in_specs = (P("grp", "row", None), P("row", None))
    return jax.shard_map(local, mesh=mesh, in_specs=in_specs, out_specs=P("row", "grp"), check_vma=False)
```

time: 94.7 us -> 90.9 us (0.960)
  the two profiles are of different devices: /device:TPU:1 before, /device:TPU:8 now
where the time goes in v6:
time: 90.9 us; the launch traced here: 90.7 us
  Pallas kernels  89 us (98%)
  local copies, waits for them, and re-layouts  1.69 us (2%)
    pallas_call x1, Pallas kernels, local(): pl.pallas_call(kernel, out_shape=jax.ShapeDtypeStruct((192, 384), F32), i...  89 us

profile of v6, /device:TPU:8, one launch (start us, length us, event | category | flops | bytes accessed | tf_op | source)
XLA Modules:
  0.0 90.7 jit_solution(1131774746629038582)
XLA Ops:
  0.0 89.0 %exchange.1 = f32[192,384]{1,0:T(8,128)} custom-call(bf16[192,6144]{1,0:T(8,128)(2,1)} %bitcast.1, bf16[192,512]{1,0:T(8,128)(2,1)} %occ_hbm.1), custom_call_target="tpu_custom_call" | custom-call | tf_op jit(solution)/shard_map/exchange/pallas_call | solution.py:300
  89.1 1.7 %copy.4 = f32[192,384]{1,0:T(8,128)} copy(f32[192,384]{1,0:T(8,128)} %exchange.1) | data formatting | bytes 589824

commit v7 on v6

--- a/solution.py
+++ b/solution.py
@@ -9,7 +9,7 @@
 F32 = jnp.float32
 BF16 = jnp.bfloat16
 
-N_SEM = 73
+N_SEM = 78
 
 
 def kernel(ints_hbm, occ_hbm, out_ref, occ, ints, hacc, hrow, hcol, pb,
@@ -71,13 +71,21 @@
     zr, zd, zo = up(zl, 1), up(zl, -1), up(zl, 2)
     east, west, north, south = at(dx=1), at(dx=-1), at(dz=1), at(dz=-1)
     PA, PB = pl.ds(0, 256), pl.ds(256, 256)
-    ALL, TOP, BOT = pl.ds(0, 192), pl.ds(0, 96), pl.ds(96, 96)
+    y_up, y_dn = at(dy=1), at(dy=-1)
+    odd = y % 2
+
+    def rows_at(first, step, size):
+        return pl.ds(pl.multiple_of(first + step * odd, 32), size)
+
+    GOT, TOP, BOT = rows_at(0, 64, 128), rows_at(0, 64, 64), rows_at(64, 64, 64)
+    LACK, LACK_TOP, LACK_BOT = rows_at(128, -128, 64), rows_at(128, -128, 32), rows_at(160, -128, 32)
+    UP, DOWN = rows_at(0, 160, 32), rows_at(32, 96, 32)
 
     def blk(bz, bx, rows, cols):
         return occ.at[bz, bx, c, rows, cols]
 
     GATHER, SIBLING, BLOCKS, SUMS = range(4)
-    half_block = blk(zl, x, ALL, PA)
+    got_block = blk(zl, x, GOT, PA)
 
     def hop(ref, to, sem=None):
         return same(ref, to, arrival() if sem is None else sem, GATHER)
@@ -85,10 +93,15 @@
     def over(ref, sem):
         return same(ref, sibling, sem, SIBLING)
 
+    def over_y(bz, bx, cols, sem):
+        hop(blk(bz, bx, UP, cols), y_up, sem)
+        hop(blk(bz, bx, DOWN, cols), y_dn, sem)
+
     sib_0, sib_1, sib_2 = arrival(), arrival(), arrival()
+    y_0, y_1 = arrival(), [arrival() for i in range(4)]
     fwd_a = [[], []]
     fwd_b = [[], []]
-    own_a, own_b = blk(zl, x, ALL, PA), blk(zl, x, ALL, PB)
+    own_a, own_b = blk(zl, x, GOT, PA), blk(zl, x, GOT, PB)
     a_e, a_w = hop(own_a, east), hop(own_a, west)
     b_n, b_s = hop(own_b, north), hop(own_b, south)
     fwd_a[0].append(hop(own_a, north))
@@ -98,51 +111,76 @@
     over(occ.at[zl, x, c], sib_0)
 
     a_2, b_2 = arrival(), arrival()
-    landed(a_e, half_block)
+    landed(a_e, got_block)
     hop(blk(zl, xl, TOP, PA), east, a_2)
-    fwd_a[0].append(hop(blk(zl, xl, ALL, PA), north))
-    fwd_a[1].append(hop(blk(zl, xl, ALL, PA), south))
-    landed(b_n, half_block)
+    over_y(zl, xl, PA, y_0)
+    fwd_a[0].append(hop(blk(zl, xl, GOT, PA), north))
+    fwd_a[1].append(hop(blk(zl, xl, GOT, PA), south))
+    landed(b_n, got_block)
     hop(blk(zd, x, TOP, PB), north, b_2)
-    fwd_b[0].append(hop(blk(zd, x, ALL, PB), east))
-    fwd_b[1].append(hop(blk(zd, x, ALL, PB), west))
-    landed(a_w, half_block)
+    over_y(zd, x, PB, y_0)
+    fwd_b[0].append(hop(blk(zd, x, GOT, PB), east))
+    fwd_b[1].append(hop(blk(zd, x, GOT, PB), west))
+    landed(a_w, got_block)
     hop(blk(zl, xr, BOT, PA), west, a_2)
-    fwd_a[0].append(hop(blk(zl, xr, ALL, PA), north))
-    fwd_a[1].append(hop(blk(zl, xr, ALL, PA), south))
-    landed(b_s, half_block)
+    over_y(zl, xr, PA, y_0)
+    fwd_a[0].append(hop(blk(zl, xr, GOT, PA), north))
+    fwd_a[1].append(hop(blk(zl, xr, GOT, PA), south))
+    landed(b_s, got_block)
     hop(blk(zr, x, BOT, PB), south, b_2)
-    fwd_b[0].append(hop(blk(zr, x, ALL, PB), east))
-    fwd_b[1].append(hop(blk(zr, x, ALL, PB), west))
-    over(blk(zl, xl, ALL, PA), sib_0)
-    over(blk(zl, xr, ALL, PA), sib_0)
-    over(blk(zd, x, ALL, PB), sib_0)
-    over(blk(zr, x, ALL, PB), sib_0)
-    landed(a_2, half_block)
-    fwd_a[0].append(hop(blk(zl, xo, ALL, PA), north))
-    fwd_a[1].append(hop(blk(zl, xo, ALL, PA), south))
-    over(blk(zl, xo, ALL, PA), sib_0)
-    landed(b_2, half_block)
-    fwd_b[0].append(hop(blk(zo, x, ALL, PB), east))
-    fwd_b[1].append(hop(blk(zo, x, ALL, PB), west))
-    over(blk(zo, x, ALL, PB), sib_0)
+    over_y(zr, x, PB, y_0)
+    fwd_b[0].append(hop(blk(zr, x, GOT, PB), east))
+    fwd_b[1].append(hop(blk(zr, x, GOT, PB), west))
+    over(blk(zl, xl, GOT, PA), sib_0)
+    over(blk(zl, xr, GOT, PA), sib_0)
+    over(blk(zd, x, GOT, PB), sib_0)
+    over(blk(zr, x, GOT, PB), sib_0)
+    landed(a_2, got_block)
+    fwd_a[0].append(hop(blk(zl, xo, GOT, PA), north))
+    fwd_a[1].append(hop(blk(zl, xo, GOT, PA), south))
+    over_y(zl, xo, PA, y_0)
+    over(blk(zl, xo, GOT, PA), sib_0)
+    landed(b_2, got_block)
+    fwd_b[0].append(hop(blk(zo, x, GOT, PB), east))
+    fwd_b[1].append(hop(blk(zo, x, GOT, PB), west))
+    over_y(zo, x, PB, y_0)
+    over(blk(zo, x, GOT, PB), sib_0)
 
     last = []
     for bx, bz, j in zip((x, xl, xr, xo), (zl, zd, zr, zo), range(4)):
         last_a, last_b = arrival(), arrival()
-        landed(fwd_a[0][j], half_block)
+        landed(fwd_a[0][j], got_block)
         hop(blk(zd, bx, TOP, PA), north, last_a)
-        over(blk(zd, bx, ALL, PA), sib_1)
-        landed(fwd_a[1][j], half_block)
+        over_y(zd, bx, PA, y_1[0])
+        landed(fwd_b[0][j], got_block)
+        hop(blk(bz, xl, TOP, PB), east, last_b)
+        over_y(bz, xl, PB, y_1[1])
+        landed(fwd_a[1][j], got_block)
         hop(blk(zr, bx, BOT, PA), south, last_a)
-        over(blk(zr, bx, ALL, PA), sib_1)
-        landed(fwd_b[0][j], half_block)
-        hop(blk(bz, xl, TOP, PB), east, last_b)
-        over(blk(bz, xl, ALL, PB), sib_1)
-        landed(fwd_b[1][j], half_block)
+        over_y(zr, bx, PA, y_1[2])
+        landed(fwd_b[1][j], got_block)
         hop(blk(bz, xr, BOT, PB), west, last_b)
-        over(blk(bz, xr, ALL, PB), sib_1)
+        over_y(bz, xr, PB, y_1[3])
+        over(blk(zd, bx, GOT, PA), sib_1)
+        over(blk(bz, xl, GOT, PB), sib_1)
+        over(blk(zr, bx, GOT, PA), sib_1)
+        over(blk(bz, xr, GOT, PB), sib_1)
         last.append((last_a, bx, last_b, bz))
+
+    landed(y_0, occ.at[0, :, 0, 0:48])
+    for bx, bz in zip((xl, xr, xo), (zd, zr, zo)):
+        over(blk(zl, bx, LACK, PA), sib_0)
+        over(blk(bz, x, LACK, PB), sib_0)
+    lack_a, lack_b = arrival(), arrival()
+    quarter = occ.at[zl, :, c, LACK, PA]
+    for i, (part, top, bot, to, sem) in enumerate((
+            (lambda rows: occ.at[zd, :, c, rows, PA], LACK_TOP, None, north, lack_a),
+            (lambda rows: occ.at[:, xl, c, rows, PB], LACK_TOP, None, east, lack_b),
+            (lambda rows: occ.at[zr, :, c, rows, PA], None, LACK_BOT, south, lack_a),
+            (lambda rows: occ.at[:, xr, c, rows, PB], None, LACK_BOT, west, lack_b))):
+        landed(y_1[i], quarter)
+        hop(part(top or bot), to, sem)
+        over(part(LACK), sib_1)
 
     def lanes(start, size):
         return pl.ds(pl.multiple_of(start, 128), size)
@@ -159,20 +197,24 @@
             total = term if total is None else total + term
         return total
 
+    for last_a, bx, last_b, bz in last:
+        landed(last_a, got_block)
+        over(blk(zo, bx, GOT, PA), sib_2)
+        landed(last_b, got_block)
+        over(blk(bz, xo, GOT, PB), sib_2)
     ints_copy.wait()
     landed(sib_0, occ.at[zl, :, 1 - c])
     hacc[:, 0:256] = part_a(zl)
     hacc[:, 256:512] = part_b(x)
+    landed(lack_a, quarter)
+    over(occ.at[zo, :, c, LACK, PA], sib_2)
+    landed(lack_b, quarter)
+    over(occ.at[:, xo, c, LACK, PB], sib_2)
     landed(sib_1, occ.at[zl])
     hacc[:, 0:256] += part_a(zd)
     hacc[:, 256:512] += part_b(xl)
     hacc[:, 0:256] += part_a(zr)
     hacc[:, 256:512] += part_b(xr)
-    for last_a, bx, last_b, bz in last:
-        landed(last_a, half_block)
-        over(blk(zo, bx, ALL, PA), sib_2)
-        landed(last_b, half_block)
-        over(blk(bz, xo, ALL, PB), sib_2)
     landed(sib_2, occ.at[zl, :, 1 - c])
     h_a = (hacc[:, 0:256] + part_a(zo)).astype(BF16)
     h_b = (hacc[:, 256:512] + part_b(xo)).astype(BF16)
@@ -188,24 +230,19 @@
             same(hcol.at[s, zl, c], in_group(d), sem, BLOCKS)
         return sem
 
-    Q = [pl.ds(48 * j, 48) for j in range(4)]
-    r_1, r_2 = [arrival(), arrival()], [arrival(), arrival()]
-    same(hrow.at[x, TOP], east, r_1[0], BLOCKS)
-    same(hrow.at[x, TOP], west, r_1[0], BLOCKS)
-    c_in = [columns_out(0)]
-    same(hrow.at[x, BOT], east, r_1[1], BLOCKS)
-    same(hrow.at[x, BOT], west, r_1[1], BLOCKS)
-    c_in += [columns_out(1), columns_out(2)]
+    UPPER, LOWER = pl.ds(0, 96), pl.ds(96, 96)
+    r_in = [arrival(), arrival()]
+    c_in = []
+    for t, half in enumerate((UPPER, LOWER)):
+        for d in (2, 1, -1):
+            same(hrow.at[x, half], at(dx=d), r_in[t], BLOCKS)
+        c_in.append(columns_out(t))
+    c_in.append(columns_out(2))
     c_sib = [arrival() for s in range(3)]
     for s in range(3):
         same(hcol.at[s, zl, c], sibling, c_sib[s], BLOCKS)
-    for t in range(2):
-        landed(r_1[t], hrow.at[x])
-        same(hrow.at[xl, Q[2 * t]], east, r_2[t], BLOCKS)
-        same(hrow.at[xr, Q[2 * t + 1]], west, r_2[t], BLOCKS)
 
     yr, yl, yo = up(y, 1), up(y, -1), up(y, 2)
-    y_up, y_dn = at(dy=1), at(dy=-1)
     hr, hl, ho = up(zh, 1), up(zh, -1), up(zh, 2)
     z_up, z_dn = at(dz=4), at(dz=-4)
     A, B = pl.ds(0, 192), pl.ds(192, 192)
@@ -235,7 +272,7 @@
         if k % 2 == 0:
             columns_in(k // 2)
         if k < 2:
-            landed(r_2[k], hrow.at[x, TOP])
+            landed(r_in[k], hrow.at[0:3, UPPER])
         product(k)
         y1[k], y2[k] = arrival(), arrival()
         pass_on(pb.at[k, yo, A], yin.at[k, 0], y_up, y1[k])

time: 90.9 us -> 92.2 us (1.014)
  the two profiles are of different devices: /device:TPU:8 before, /device:TPU:1 now
where the time goes in v7:
time: 92.2 us; the launch traced here: 90.8 us
  Pallas kernels  89.1 us (97%)
  local copies, waits for them, and re-layouts  1.69 us (2%)
    pallas_call x1, Pallas kernels, local(): pl.pallas_call(kernel, out_shape=jax.ShapeDtypeStruct((192, 384), F32), i...  89.1 us

profile of v7, /device:TPU:1, one launch (start us, length us, event | category | flops | bytes accessed | tf_op | source)
XLA Modules:
  0.0 90.8 jit_solution(9033486259093241331)
XLA Ops:
  0.0 89.1 %exchange.1 = f32[192,384]{1,0:T(8,128)} custom-call(bf16[192,6144]{1,0:T(8,128)(2,1)} %bitcast.1, bf16[192,512]{1,0:T(8,128)(2,1)} %occ_hbm.1), custom_call_target="tpu_custom_call" | custom-call | tf_op jit(solution)/shard_map/exchange/pallas_call | solution.py:337
  89.1 1.7 %copy.4 = f32[192,384]{1,0:T(8,128)} copy(f32[192,384]{1,0:T(8,128)} %exchange.1) | data formatting | bytes 589824

commit v8 on v6

--- a/solution.py
+++ b/solution.py
@@ -9,7 +9,7 @@
 F32 = jnp.float32
 BF16 = jnp.bfloat16
 
-N_SEM = 73
+N_SEM = 71
 
 
 def kernel(ints_hbm, occ_hbm, out_ref, occ, ints, hacc, hrow, hcol, pb,
@@ -163,16 +163,16 @@
     landed(sib_0, occ.at[zl, :, 1 - c])
     hacc[:, 0:256] = part_a(zl)
     hacc[:, 256:512] = part_b(x)
+    for last_a, bx, last_b, bz in last:
+        landed(last_a, half_block)
+        over(blk(zo, bx, ALL, PA), sib_2)
+        landed(last_b, half_block)
+        over(blk(bz, xo, ALL, PB), sib_2)
     landed(sib_1, occ.at[zl])
     hacc[:, 0:256] += part_a(zd)
     hacc[:, 256:512] += part_b(xl)
     hacc[:, 0:256] += part_a(zr)
     hacc[:, 256:512] += part_b(xr)
-    for last_a, bx, last_b, bz in last:
-        landed(last_a, half_block)
-        over(blk(zo, bx, ALL, PA), sib_2)
-        landed(last_b, half_block)
-        over(blk(bz, xo, ALL, PB), sib_2)
     landed(sib_2, occ.at[zl, :, 1 - c])
     h_a = (hacc[:, 0:256] + part_a(zo)).astype(BF16)
     h_b = (hacc[:, 256:512] + part_b(xo)).astype(BF16)
@@ -188,21 +188,17 @@
             same(hcol.at[s, zl, c], in_group(d), sem, BLOCKS)
         return sem
 
-    Q = [pl.ds(48 * j, 48) for j in range(4)]
-    r_1, r_2 = [arrival(), arrival()], [arrival(), arrival()]
-    same(hrow.at[x, TOP], east, r_1[0], BLOCKS)
-    same(hrow.at[x, TOP], west, r_1[0], BLOCKS)
-    c_in = [columns_out(0)]
-    same(hrow.at[x, BOT], east, r_1[1], BLOCKS)
-    same(hrow.at[x, BOT], west, r_1[1], BLOCKS)
-    c_in += [columns_out(1), columns_out(2)]
+    UPPER, LOWER = pl.ds(0, 96), pl.ds(96, 96)
+    r_in = [arrival(), arrival()]
+    c_in = []
+    for t, half in enumerate((UPPER, LOWER)):
+        for d in (2, 1, -1):
+            same(hrow.at[x, half], at(dx=d), r_in[t], BLOCKS)
+        c_in.append(columns_out(t))
+    c_in.append(columns_out(2))
     c_sib = [arrival() for s in range(3)]
     for s in range(3):
         same(hcol.at[s, zl, c], sibling, c_sib[s], BLOCKS)
-    for t in range(2):
-        landed(r_1[t], hrow.at[x])
-        same(hrow.at[xl, Q[2 * t]], east, r_2[t], BLOCKS)
-        same(hrow.at[xr, Q[2 * t + 1]], west, r_2[t], BLOCKS)
 
     yr, yl, yo = up(y, 1), up(y, -1), up(y, 2)
     y_up, y_dn = at(dy=1), at(dy=-1)
@@ -235,7 +231,7 @@
         if k % 2 == 0:
             columns_in(k // 2)
         if k < 2:
-            landed(r_2[k], hrow.at[x, TOP])
+            landed(r_in[k], hrow.at[0:3, UPPER])
         product(k)
         y1[k], y2[k] = arrival(), arrival()
         pass_on(pb.at[k, yo, A], yin.at[k, 0], y_up, y1[k])
@@ -286,8 +282,8 @@
             out_ref[first:first + 48, 192 + 64 * s:192 + 64 * s + 64] = v[:, 64:128]
 
     steps = {"F": y_first, "S": y_second, "L": y_last, "f": z_first, "s": z_second, "l": z_last}
-    for part in ("F0F1S0F2S1F3L0S2F4", "L1S3F5f0L2f1S4L3S5f2s0L4s1f3L5",
-                 "s2l0f4f5s3l1s4l2s5l3l4l5"):
+    for part in ("F0F1S0F2S1F3L0S2F4L1S3f0F5L2f1S4", "L3s0S5f2L4s1f3L5s2f4f5l0",
+                 "s3l1s4l2s5l3l4l5"):
         for j in range(0, len(part), 2):
             steps[part[j]](int(part[j + 1]))
     for group, ref in ((GATHER, occ.at[0:3, 0:3, :, 0:160]), (SIBLING, occ.at[:, :, 0]),

time: 90.9 us -> 91.3 us (level)
  the two profiles are of different devices: /device:TPU:8 before, /device:TPU:1 now
where the time goes in v8:
time: 91.3 us; the launch traced here: 91.1 us
  Pallas kernels  89.4 us (98%)
  local copies, waits for them, and re-layouts  1.69 us (2%)
    pallas_call x1, Pallas kernels, local(): pl.pallas_call(kernel, out_shape=jax.ShapeDtypeStruct((192, 384), F32), i...  89.4 us

profile of v8, /device:TPU:1, one launch (start us, length us, event | category | flops | bytes accessed | tf_op | source)
XLA Modules:
  0.0 91.1 jit_solution(3634092265905143680)
XLA Ops:
  0.0 89.4 %exchange.1 = f32[192,384]{1,0:T(8,128)} custom-call(bf16[192,6144]{1,0:T(8,128)(2,1)} %bitcast.1, bf16[192,512]{1,0:T(8,128)(2,1)} %occ_hbm.1), custom_call_target="tpu_custom_call" | custom-call | tf_op jit(solution)/shard_map/exchange/pallas_call | solution.py:296
  89.4 1.7 %copy.4 = f32[192,384]{1,0:T(8,128)} copy(f32[192,384]{1,0:T(8,128)} %exchange.1) | data formatting | bytes 589824

commit v9 on v6

--- a/solution.py
+++ b/solution.py
@@ -163,16 +163,16 @@
     landed(sib_0, occ.at[zl, :, 1 - c])
     hacc[:, 0:256] = part_a(zl)
     hacc[:, 256:512] = part_b(x)
+    for last_a, bx, last_b, bz in last:
+        landed(last_a, half_block)
+        over(blk(zo, bx, ALL, PA), sib_2)
+        landed(last_b, half_block)
+        over(blk(bz, xo, ALL, PB), sib_2)
     landed(sib_1, occ.at[zl])
     hacc[:, 0:256] += part_a(zd)
     hacc[:, 256:512] += part_b(xl)
     hacc[:, 0:256] += part_a(zr)
     hacc[:, 256:512] += part_b(xr)
-    for last_a, bx, last_b, bz in last:
-        landed(last_a, half_block)
-        over(blk(zo, bx, ALL, PA), sib_2)
-        landed(last_b, half_block)
-        over(blk(bz, xo, ALL, PB), sib_2)
     landed(sib_2, occ.at[zl, :, 1 - c])
     h_a = (hacc[:, 0:256] + part_a(zo)).astype(BF16)
     h_b = (hacc[:, 256:512] + part_b(xo)).astype(BF16)
@@ -286,8 +286,8 @@
             out_ref[first:first + 48, 192 + 64 * s:192 + 64 * s + 64] = v[:, 64:128]
 
     steps = {"F": y_first, "S": y_second, "L": y_last, "f": z_first, "s": z_second, "l": z_last}
-    for part in ("F0F1S0F2S1F3L0S2F4", "L1S3F5f0L2f1S4L3S5f2s0L4s1f3L5",
-                 "s2l0f4f5s3l1s4l2s5l3l4l5"):
+    for part in ("F0F1S0F2S1F3L0S2F4L1S3f0F5L2f1S4", "L3s0S5f2L4s1f3L5s2f4f5l0",
+                 "s3l1s4l2s5l3l4l5"):
         for j in range(0, len(part), 2):
             steps[part[j]](int(part[j + 1]))
     for group, ref in ((GATHER, occ.at[0:3, 0:3, :, 0:160]), (SIBLING, occ.at[:, :, 0]),

time: 90.9 us -> 89.9 us (0.989)
  the two profiles are of different devices: /device:TPU:8 before, /device:TPU:1 now
where the time goes in v9:
time: 89.9 us; the launch traced here: 89.7 us
  Pallas kernels  88 us (98%)
  local copies, waits for them, and re-layouts  1.69 us (2%)
    pallas_call x1, Pallas kernels, local(): pl.pallas_call(kernel, out_shape=jax.ShapeDtypeStruct((192, 384), F32), i...  88 us

profile of v9, /device:TPU:1, one launch (start us, length us, event | category | flops | bytes accessed | tf_op | source)
XLA Modules:
  0.0 89.7 jit_solution(7809529528532326468)
XLA Ops:
  0.0 88.0 %exchange.1 = f32[192,384]{1,0:T(8,128)} custom-call(bf16[192,6144]{1,0:T(8,128)(2,1)} %bitcast.1, bf16[192,512]{1,0:T(8,128)(2,1)} %occ_hbm.1), custom_call_target="tpu_custom_call" | custom-call | tf_op jit(solution)/shard_map/exchange/pallas_call | solution.py:300
  88.1 1.7 %copy.4 = f32[192,384]{1,0:T(8,128)} copy(f32[192,384]{1,0:T(8,128)} %exchange.1) | data formatting | bytes 589824

commit v10 on v9

--- a/solution.py
+++ b/solution.py
@@ -216,7 +216,6 @@
         landed(c_in[s], hcol.at[s, 0:3, c])
         for d in (1, 3, 2):
             same(hcol.at[s, up(zl, d), c], sibling, c_sib[s], BLOCKS)
-        landed(c_sib[s], hcol.at[s, :, 1 - c])
 
     def product(k):
         s, t = k // 2, k % 2
@@ -233,7 +232,7 @@
 
     def y_first(k):
         if k % 2 == 0:
-            columns_in(k // 2)
+            landed(c_sib[k // 2], hcol.at[k // 2, :, 1 - c])
         if k < 2:
             landed(r_2[k], hrow.at[x, TOP])
         product(k)
@@ -285,9 +284,8 @@
             out_ref[first:first + 48, 64 * s:64 * s + 64] = v[:, 0:64]
             out_ref[first:first + 48, 192 + 64 * s:192 + 64 * s + 64] = v[:, 64:128]
 
-    steps = {"F": y_first, "S": y_second, "L": y_last, "f": z_first, "s": z_second, "l": z_last}
-    for part in ("F0F1S0F2S1F3L0S2F4L1S3f0F5L2f1S4", "L3s0S5f2L4s1f3L5s2f4f5l0",
-                 "s3l1s4l2s5l3l4l5"):
+    steps = {"C": columns_in, "F": y_first, "S": y_second, "L": y_last, "f": z_first, "s": z_second, "l": z_last}
+    for part in ("C0F0F1S0C1F2S1F3L0S2C2L1F4f0S3F5L2f1S4L3", "s0S5f2L4s1f3L5s2f4f5l0s3l1s4l2s5l3l4l5"):
         for j in range(0, len(part), 2):
             steps[part[j]](int(part[j + 1]))
     for group, ref in ((GATHER, occ.at[0:3, 0:3, :, 0:160]), (SIBLING, occ.at[:, :, 0]),

time: 89.9 us -> 90.8 us (1.010)
  no operation moved by 1% of the time
where the time goes in v10:
time: 90.8 us; the launch traced here: 90.6 us
  Pallas kernels  88.9 us (98%)
  local copies, waits for them, and re-layouts  1.69 us (2%)
    pallas_call x1, Pallas kernels, local(): pl.pallas_call(kernel, out_shape=jax.ShapeDtypeStruct((192, 384), F32), i...  88.9 us

profile of v10, /device:TPU:1, one launch (start us, length us, event | category | flops | bytes accessed | tf_op | source)
XLA Modules:
  0.0 90.6 jit_solution(11719881584300064092)
XLA Ops:
  0.0 88.9 %exchange.1 = f32[192,384]{1,0:T(8,128)} custom-call(bf16[192,6144]{1,0:T(8,128)(2,1)} %bitcast.1, bf16[192,512]{1,0:T(8,128)(2,1)} %occ_hbm.1), custom_call_target="tpu_custom_call" | custom-call | tf_op jit(solution)/shard_map/exchange/pallas_call | solution.py:298
  88.9 1.7 %copy.4 = f32[192,384]{1,0:T(8,128)} copy(f32[192,384]{1,0:T(8,128)} %exchange.1) | data formatting | bytes 589824
